TPU v7x, 256 devices: a whole 4x4x8 slice. The times are simulated.
256 devices in a mesh: sky: 16 (over x, y), freq: 16 (over z, core).
Axes of the slice: x: 4, y: 4, z: 8, core: 2. Of those that a mesh axis runs over, the one named last changes fastest.
Arguments:
- pieces: bfloat16 [128, 128, 128, 128], P('sky', 'freq'), may hold values from -120 to 120
- beam: bfloat16 [128, 128, 128], P('sky'), may hold values from 0.099609375 to 1
- destination: int32 [128], P('sky'), may hold values from 0 to 63, as said below
- clip_tenths: int32 [3, 4], replicated, may hold values from 30 to 60
Outputs:
- significance: float32 [128, 2048, 512], P('freq', 'sky')
Inputs may be any that keep to these rules, and one draw needn't show every extreme that they name: Among the 8 pieces of one index of sky, at most 2 have destinations in one tile, that is with equal destination // 4. In every draw some tile receives exactly 2 pieces from every index of sky.
All inputs are finite; a program needn't handle non-finite values.
Results may differ from a plain program's by a relative error of at most 0.0036.
Values may be sent and summed in bfloat16 or wider, within the bound.
A program may use at most 128 MiB of HBM per device.

v0:
```python
import jax
import jax.numpy as jnp
from jax import lax
from jax.sharding import PartitionSpec as P

ROWB = 1
COLB = 4
RIM = 8
EDGE = 7
KERNELS = 3


REGULARIZER = 0.05
EPSILON = 1e-06
KERNEL_FWHM = (3.0, 6.0, 9.0)
HALF_WIDTHS = (0, 1, 3, 7)


def extended(block, sides, width):
    for axis, dim in sides:
        count = lax.axis_size(axis)
        forward = [(i, i + 1) for i in range(count - 1)]
        backward = [(target, source) for source, target in forward]
        low = lax.ppermute(
            lax.slice_in_dim(block, block.shape[dim] - width, None, axis=dim), axis, forward
        )
        high = lax.ppermute(lax.slice_in_dim(block, 0, width, axis=dim), axis, backward)
        block = jnp.concatenate([low, block, high], axis=dim)
    return block


def kernel_taps(kernel):
    offsets = jnp.arange(-RIM, RIM + 1).astype(jnp.float32)
    sigma = KERNEL_FWHM[kernel] / 2.3548
    return jnp.exp(-offsets * offsets / (2.0 * sigma * sigma)).astype(jnp.bfloat16)


def band_matrix(weights, rows_out, rows_in, shift):
    outer = jnp.arange(rows_out)[:, None]
    inner = jnp.arange(rows_in)[None, :]
    offset = inner - shift - outer
    inside = jnp.abs(offset) <= RIM
    picked = weights[jnp.clip(offset + RIM, 0, 2 * RIM)]
    return jnp.where(inside, picked, jnp.zeros_like(picked))


def smooth(padded, kernel):
    weights = kernel_taps(kernel)
    tall = padded.shape[1] - 2 * RIM
    broad = padded.shape[2]
    across_matrix = band_matrix(weights, broad, broad, 0)
    down_matrix = band_matrix(weights, tall, tall + 2 * RIM, RIM)
    across = jnp.einsum(
        "cyx,zx->cyz", padded, across_matrix, preferred_element_type=jnp.float32
    ).astype(jnp.bfloat16)
    return jnp.einsum(
        "vy,cyz->cvz", down_matrix, across, preferred_element_type=jnp.float32
    ).astype(jnp.bfloat16)


def boxcars(layer):
    channels = layer.shape[0] - 2 * EDGE
    running = layer[EDGE : EDGE + channels].astype(jnp.float32)
    found = [running]
    for step in range(1, EDGE + 1):
        running = (
            running
            + layer[EDGE - step : EDGE - step + channels].astype(jnp.float32)
            + layer[EDGE + step : EDGE + step + channels].astype(jnp.float32)
        )
        if step in HALF_WIDTHS:
            found.append(running)
    return found


def kernel_boxcars(layer):
    found = boxcars(layer)
    power = jnp.stack([jnp.sum(item * item, axis=(1, 2)) for item in found])
    return (found, power)


def raise_score(best, found, totals, thresholds, cells):
    noise_level = jnp.sqrt(totals / cells + EPSILON)
    factor = 10.0 / (thresholds.astype(jnp.float32)[:, None] * noise_level)
    for width, running in enumerate(found):
        best = jnp.maximum(best, jnp.abs(running) * factor[width][:, None, None])
    return best


def owner_tables(beams_in, labels_in, tile_blocks):
    onehot = labels_in[None, :] == jnp.arange(tile_blocks)[:, None]
    beam_wide = beams_in.astype(jnp.float32)
    coverage = (
        jnp.einsum(
            "bs,syx->byx",
            onehot.astype(jnp.float32),
            beam_wide * beam_wide,
            precision=lax.Precision.HIGHEST,
        )
        + REGULARIZER
    )
    return (onehot.astype(jnp.bfloat16), coverage)


def block_values(onehot, coverage, arrived):
    numerator = jnp.einsum("bs,scyx->bcyx", onehot, arrived, preferred_element_type=jnp.float32)
    return (numerator / coverage[:, None]).astype(jnp.bfloat16)


def shards(pieces, beam, destination, clip_tenths):
    sky_count = lax.axis_size("sky")
    piece_count, channels, block_size, _ = pieces.shape
    tile_blocks = ROWB * COLB
    capacity = max(2, 2 * piece_count // sky_count)
    slot_total = sky_count * capacity
    owners = destination // tile_blocks
    numbering = jnp.arange(piece_count)
    earlier = (owners[None, :] == owners[:, None]) & (numbering[None, :] < numbering[:, None])
    position = jnp.sum(earlier.astype(jnp.int32), axis=1)
    slot_index = owners * capacity + position
    weighted = (beam[:, None].astype(jnp.float32) * pieces.astype(jnp.float32)).astype(jnp.bfloat16)
    outgoing = (
        jnp.zeros((slot_total, channels, block_size, block_size), jnp.bfloat16)
        .at[slot_index]
        .set(weighted)
    )
    beams_out = (
        jnp.zeros((slot_total, block_size, block_size), jnp.bfloat16).at[slot_index].set(beam)
    )
    labels_out = (
        jnp.full((slot_total,), -1, jnp.int32).at[slot_index].set(destination % tile_blocks)
    )
    arrived, beams_in, labels_in = (
        lax.all_to_all(outgoing, "sky", split_axis=0, concat_axis=0, tiled=True),
        lax.all_to_all(beams_out, "sky", split_axis=0, concat_axis=0, tiled=True),
        lax.all_to_all(labels_out, "sky", split_axis=0, concat_axis=0, tiled=True),
    )
    onehot, coverage = owner_tables(beams_in, labels_in, tile_blocks)
    tile_values = block_values(onehot, coverage, arrived)
    combined = tile_values.reshape(ROWB, COLB, channels, block_size, block_size).transpose(
        2, 0, 3, 1, 4
    )
    combined = combined.reshape(channels, ROWB * block_size, COLB * block_size)
    padded = extended(combined, (("sky", 1),), RIM)
    smoothed = jnp.stack([smooth(padded, kernel) for kernel in range(KERNELS)])
    planes = extended(smoothed, (("freq", 1),), EDGE)
    cells = float(sky_count * ROWB * block_size * COLB * block_size)
    best = jnp.zeros((channels, ROWB * block_size, COLB * block_size), jnp.float32)
    results = [kernel_boxcars(planes[kernel]) for kernel in range(KERNELS)]
    powers = jnp.stack([item[1] for item in results])
    totals = lax.psum(powers, "sky")
    for kernel in range(KERNELS):
        best = raise_score(best, results[kernel][0], totals[kernel], clip_tenths[kernel], cells)
    return best


def solution(mesh):
    return jax.shard_map(
        shards,
        mesh=mesh,
        in_specs=(P("sky", "freq", None, None), P("sky", None, None), P("sky"), P()),
        out_specs=P("freq", "sky", None),
        check_vma=False,
    )
```

profile of v0, /device:TPU:1, one launch (start us, length us, event | category | flops | bytes accessed | tf_op | source)
XLA Modules:
  0.0 321.2 jit_solution(16188896289594419364)
XLA Ops:
  2.2 7.6 %all-to-all-start = ((s32[16,2,1]{1,2,0:T(1,128)}), s32[16,2,1]{1,2,0:T(1,128)S(1)}, u32[]{:S(2)}, u32[]{:S(2)}) async-start(s32[16,2,1]{1,2,0:T(1,128)} %bitcast), calls=%async_computation | async-start | bytes 16384 | tf_op jit(solution)/shard_map/all_to_all | solution.py:136
  11.0 2.4 scatter_fusion.1
  13.4 2.8 all-to-all-done
  16.2 3.9 %all-to-all-start.2 = ((bf16[32,128,128]{2,1,0:T(8,128)(2,1)}), bf16[32,128,128]{2,1,0:T(8,128)(2,1)S(1)}, u32[]{:S(2)}, u32[]{:S(2)}) async-start(bf16[32,128,128]{2,1,0:T(8,128)(2,1)} %scatter_fusion.1), calls=%async_computation.2 | async-start | bytes 2097152 | tf_op jit(solution)/shard_map/all_to_all | solution.py:135
  20.1 2.2 multiply_convert_fusion
  22.3 5.3 %broadcast_in_dim.12 = bf16[32,8,128,128]{3,2,1,0:T(8,128)(2,1)} broadcast(bf16[]{:T(256)} %constant.32.clone.1), dimensions={} | broadcast | bytes 8388610 | tf_op jit(solution)/shard_map/broadcast_in_dim | solution.py:123
  27.7 5.0 %scatter_fusion = bf16[32,8,128,128]{3,2,1,0:T(8,128)(2,1)} fusion(bf16[32,8,128,128]{3,2,1,0:T(8,128)(2,1)} %broadcast_in_dim.12, s32[8]{0:T(128)S(1)} %compare_select_fusion.2, bf16[8,8,128,128]{3,2,1,0:T(8,128)(2,1)S(1)} %multiply_convert_fusion), kind=kCustom, calls=%fused_computation.1 | custom fusion | bytes 6291488 | tf_op jit(solution)/shard_map/scatter | solution.py:125
  32.7 2.4 all-to-all-done.2
  35.1 4.7 %all-to-all-start.1 = ((bf16[32,8,128,128]{3,2,1,0:T(8,128)(2,1)}), bf16[32,8,128,128]{3,2,1,0:T(8,128)(2,1)}, u32[]{:S(2)}, u32[]{:S(2)}) async-start(bf16[32,8,128,128]{3,2,1,0:T(8,128)(2,1)} %scatter_fusion), calls=%async_computation.1 | async-start | bytes 16777216 | tf_op jit(solution)/shard_map/all_to_all | solution.py:134
  45.6 120.4 %all-to-all-done.1 = bf16[32,8,128,128]{3,2,1,0:T(8,128)(2,1)} async-done(((bf16[32,8,128,128]{3,2,1,0:T(8,128)(2,1)}), bf16[32,8,128,128]{3,2,1,0:T(8,128)(2,1)}, u32[]{:S(2)}, u32[]{:S(2)}) %all-to-all-start.1) | async-done | bytes 8388640 | tf_op jit(solution)/shard_map/all_to_all | solution.py:134
  166.0 8.3 %fusion.54 = bf16[8,1,128,4,128]{4,3,2,0,1:T(4,128)(2,1)S(1)} fusion(f32[4,128,128]{2,0,1:T(4,128)S(1)} %fusion.25, bf16[32,8,128,128]{3,2,1,0:T(8,128)(2,1)} %all-to-all-done.1, s32[32]{0:T(128)S(1)} %eq.33), kind=kOutput, calls=%fused_computation.165 | convolution fusion | flops 34603136 | bytes 9699456 | tf_op jit(solution)/shard_map/bs,scyx->bcyx/dot_general | solution.py:106
  177.7 3.4 %collective-permute-done.1 = bf16[8,8,512]{2,1,0:T(8,128)(2,1)S(1)} collective-permute-done((bf16[8,8,512]{2,1,0:T(8,128)(2,1)S(1)}, bf16[8,8,512]{2,1,0:T(8,128)(2,1)S(1)}, u32[]{:S(2)}, u32[]{:S(2)}) %collective-permute-start.1) | collective-permute-done | bytes 65568 | tf_op jit(solution)/shard_map/ppermute | solution.py:27
  181.1 12.3 %convolution_convert_fusion.4 = bf16[8,512,128]{2,1,0:T(8,128)(2,1)S(1)} fusion(bf16[8,144,512]{2,1,0:T(8,128)(2,1)S(1)} %constant_dynamic-update-slice_fusion, bf16[]{:T(256)} %bitcast.61, bf16[]{:T(256)} %bitcast.62, bf16[]{:T(256)} %bitcast.63, bf16[]{:T(256)} %bitcast.64, bf16[]{:T(256)} %bitcast.65, bf16[]{:T(256)} %bitcast.67, bf16[]{:T(256)} %bitcast.66, ...), kind=kOutput, calls=%fused_computation.93 | convolution fusion | flops 767873024 | bytes 2228834 | tf_op jit(solution)/shard_map/vy,cyz->cvz/dot_general | solution.py:56
  193.4 12.2 %convolution_convert_fusion.5 = bf16[8,512,128]{2,1,0:T(8,128)(2,1)S(1)} fusion(bf16[8,144,512]{2,1,0:T(8,128)(2,1)S(1)} %constant_dynamic-update-slice_fusion, bf16[]{:T(256)} %bitcast.26, bf16[]{:T(256)} %bitcast.27, bf16[]{:T(256)} %bitcast.28, bf16[]{:T(256)} %bitcast.29, bf16[]{:T(256)} %bitcast.30, bf16[]{:T(256)} %bitcast.32, bf16[]{:T(256)} %bitcast.31, ...), kind=kOutput, calls=%fused_computation.94 | convolution fusion | flops 767873024 | bytes 2228834 | tf_op jit(solution)/shard_map/vy,cyz->cvz/dot_general | solution.py:56
  205.7 13.5 %convolution_convert_fusion.3 = bf16[8,512,128]{2,1,0:T(8,128)(2,1)S(1)} fusion(bf16[8,144,512]{2,1,0:T(8,128)(2,1)} %copy-done.6, bf16[]{:T(256)} %bitcast.84, bf16[]{:T(256)} %bitcast.85, bf16[]{:T(256)} %bitcast.86, bf16[]{:T(256)} %bitcast.87, bf16[]{:T(256)} %bitcast.88, bf16[]{:T(256)} %bitcast.90, bf16[]{:T(256)} %bitcast.89, bf16[]{:T(256)} %bitcast.74, ...), kind=kOutput, calls=%fused_computation.92 | convolution fusion | flops 767873024 | bytes 2228834 | tf_op jit(solution)/shard_map/vy,cyz->cvz/dot_general | solution.py:56
  220.8 11.5 %collective-permute-start.2 = (bf16[3,7,128,512]{2,3,1,0:T(8,128)(2,1)S(1)}, bf16[3,7,128,512]{2,3,1,0:T(8,128)(2,1)S(1)}, u32[]{:S(2)}, u32[]{:S(2)}) collective-permute-start(bf16[3,7,128,512]{2,3,1,0:T(8,128)(2,1)S(1)} %get-tuple-element.31), channel_id=1, source_target_pairs={{0,1},{1,2},{2,3},{3,4},{4,5},{5,6},{6,7},{7,8},{8,9},{9,10},{10,1... | collective-permute-start | bytes 8257544 | tf_op jit(solution)/shard_map/ppermute | solution.py:24
  234.4 27.8 %collective-permute-done.2 = bf16[3,7,128,512]{2,3,1,0:T(8,128)(2,1)S(1)} collective-permute-done((bf16[3,7,128,512]{2,3,1,0:T(8,128)(2,1)S(1)}, bf16[3,7,128,512]{2,3,1,0:T(8,128)(2,1)S(1)}, u32[]{:S(2)}, u32[]{:S(2)}) %collective-permute-start.2) | collective-permute-done | bytes 2752544 | tf_op jit(solution)/shard_map/ppermute | solution.py:24
  262.2 4.4 %collective-permute-done.3 = bf16[3,7,128,512]{2,3,1,0:T(8,128)(2,1)S(1)} collective-permute-done((bf16[3,7,128,512]{2,3,1,0:T(8,128)(2,1)S(1)}, bf16[3,7,128,512]{2,3,1,0:T(8,128)(2,1)S(1)}, u32[]{:S(2)}, u32[]{:S(2)}) %collective-permute-start.3) | collective-permute-done | bytes 2752544 | tf_op jit(solution)/shard_map/ppermute | solution.py:27
  269.1 3.1 multiply_reduce_fusion.8
  272.2 3.6 %multiply_reduce_fusion.7 = (f32[8]{0:T(128)S(1)}, f32[8,128,512]{1,2,0:T(8,128)S(1)}, f32[8]{0:T(128)S(1)}, f32[8,128,512]{1,2,0:T(8,128)}) fusion(bf16[3,15,128,512]{2,3,1,0:T(8,128)(2,1)S(1)} %get-tuple-element.30, bf16[3,15,128,512]{2,3,1,0:T(8,128)(2,1)S(1)} %get-tuple-element.29, bf16[8,512,128]{2,1,0:T(8,128)(2,1)S(1)} %convolution_convert_fusion.5, ...), kind=kLoop, calls=%fused_computation.85 | loop fusion | flops 17301488 | bytes 22020160 | tf_op jit(solution)/shard_map/reduce_sum | solution.py:78
  275.8 4.1 %multiply_reduce_fusion.6 = (f32[8]{0:T(128)S(1)}, f32[8,128,512]{1,2,0:T(8,128)}, f32[8]{0:T(128)S(1)}, f32[8,128,512]{1,2,0:T(8,128)}) fusion(bf16[3,15,128,512]{2,3,1,0:T(8,128)(2,1)S(1)} %get-tuple-element.30, bf16[3,15,128,512]{2,3,1,0:T(8,128)(2,1)S(1)} %get-tuple-element.29, f32[8,128,512]{1,2,0:T(8,128)S(1)} %get-tuple-element.12, ...), kind=kLoop, calls=%fused_computation.84 | loop fusion | flops 18874352 | bytes 25165888 | tf_op jit(solution)/shard_map/reduce_sum | solution.py:78
  280.0 29.0 %psum.7 = f32[3,4,8]{2,1,0:T(4,128)S(1)} all-reduce(f32[3,4,8]{2,1,0:T(4,128)S(1)} %pad_maximum_fusion.2), channel_id=1, replica_groups=mesh['sky'=16,'freq'=16] {'sky'}, use_global_device_ids=true, to_apply=%region_16.17 | all-reduce | flops 96 | bytes 768 | tf_op jit(solution)/shard_map/psum | solution.py:151
  309.1 9.2 %fusion.14 = f32[8,128,512]{1,2,0:T(8,128)} fusion(f32[8,128,512]{1,2,0:T(8,128)} %get-tuple-element.26, f32[8,128,512]{1,2,0:T(8,128)} %copy-done.2, f32[8,128,512]{1,2,0:T(8,128)} %get-tuple-element.28, f32[8,128,512]{1,2,0:T(8,128)} %copy-done.3, f32[8,128,512]{1,2,0:T(8,128)} %get-tuple-element.14, f32[8,128,512]{1,2,0:T(8,128)} %copy-done.4, ...), kind=kLoop, calls=%fused_computation.31 | loop fusion | flops 26738688 | bytes 24117632 | tf_op jit(solution)/shard_map/max | solution.py:86
  318.3 2.9 copy.18
  (56 shorter events, 18.7 us)
Async XLA Ops:
  0.0 20.1 %copy-start.5 = (bf16[8,128,128]{2,1,0:T(8,128)(2,1)S(1)}, bf16[8,128,128]{2,1,0:T(8,128)(2,1)}, u32[]{:S(2)}) copy-start(bf16[8,128,128]{2,1,0:T(8,128)(2,1)} %param.5) | copy-start | bytes 786436
  2.2 14.0 %all-to-all-start = ((s32[16,2,1]{1,2,0:T(1,128)}), s32[16,2,1]{1,2,0:T(1,128)S(1)}, u32[]{:S(2)}, u32[]{:S(2)}) async-start(s32[16,2,1]{1,2,0:T(1,128)} %bitcast), calls=%async_computation | async-start | bytes 16384 | tf_op jit(solution)/shard_map/all_to_all | solution.py:136
  16.2 18.9 %all-to-all-start.2 = ((bf16[32,128,128]{2,1,0:T(8,128)(2,1)}), bf16[32,128,128]{2,1,0:T(8,128)(2,1)S(1)}, u32[]{:S(2)}, u32[]{:S(2)}) async-start(bf16[32,128,128]{2,1,0:T(8,128)(2,1)} %scatter_fusion.1), calls=%async_computation.2 | async-start | bytes 2097152 | tf_op jit(solution)/shard_map/all_to_all | solution.py:135
  35.1 130.9 %all-to-all-start.1 = ((bf16[32,8,128,128]{3,2,1,0:T(8,128)(2,1)}), bf16[32,8,128,128]{3,2,1,0:T(8,128)(2,1)}, u32[]{:S(2)}, u32[]{:S(2)}) async-start(bf16[32,8,128,128]{3,2,1,0:T(8,128)(2,1)} %scatter_fusion), calls=%async_computation.1 | async-start | bytes 16777216 | tf_op jit(solution)/shard_map/all_to_all | solution.py:134
  174.7 2.8 collective-permute-start
  176.1 5.0 %collective-permute-start.1 = (bf16[8,8,512]{2,1,0:T(8,128)(2,1)S(1)}, bf16[8,8,512]{2,1,0:T(8,128)(2,1)S(1)}, u32[]{:S(2)}, u32[]{:S(2)}) collective-permute-start(bf16[8,8,512]{2,1,0:T(8,128)(2,1)S(1)} %get-tuple-element.33), channel_id=1, source_target_pairs={{16,0},{32,16},{48,32},{64,48},{80,64},{96,80},{112,96},{128,112},... | collective-permute-start | bytes 196616 | tf_op jit(solution)/shard_map/ppermute | solution.py:27
  181.1 12.4 %copy-start.6 = (bf16[8,144,512]{2,1,0:T(8,128)(2,1)}, bf16[8,144,512]{2,1,0:T(8,128)(2,1)S(1)}, u32[]{:S(2)}) copy-start(bf16[8,144,512]{2,1,0:T(8,128)(2,1)S(1)} %constant_dynamic-update-slice_fusion) | copy-start | bytes 3538948
  219.5 14.9 %copy-start.7 = (s32[3,4]{1,0:T(4,128)S(1)}, s32[3,4]{1,0:T(4,128)}, u32[]{:S(2)}) copy-start(s32[3,4]{1,0:T(4,128)} %param.7) | copy-start | bytes 148
  220.8 41.4 %collective-permute-start.2 = (bf16[3,7,128,512]{2,3,1,0:T(8,128)(2,1)S(1)}, bf16[3,7,128,512]{2,3,1,0:T(8,128)(2,1)S(1)}, u32[]{:S(2)}, u32[]{:S(2)}) collective-permute-start(bf16[3,7,128,512]{2,3,1,0:T(8,128)(2,1)S(1)} %get-tuple-element.31), channel_id=1, source_target_pairs={{0,1},{1,2},{2,3},{3,4},{4,5},{5,6},{6,7},{7,8},{8,9},{9,10},{10,1... | collective-permute-start | bytes 8257544 | tf_op jit(solution)/shard_map/ppermute | solution.py:24
  232.3 34.4 %collective-permute-start.3 = (bf16[3,7,128,512]{2,3,1,0:T(8,128)(2,1)S(1)}, bf16[3,7,128,512]{2,3,1,0:T(8,128)(2,1)S(1)}, u32[]{:S(2)}, u32[]{:S(2)}) collective-permute-start(bf16[3,7,128,512]{2,3,1,0:T(8,128)(2,1)S(1)} %get-tuple-element.32), channel_id=1, source_target_pairs={{1,0},{2,1},{3,2},{4,3},{5,4},{6,5},{7,6},{8,7},{9,8},{10,9},{11,1... | collective-permute-start | bytes 8257544 | tf_op jit(solution)/shard_map/ppermute | solution.py:27
  267.8 8.0 %copy-start = (bf16[3,15,128,512]{2,3,1,0:T(8,128)(2,1)}, bf16[3,15,128,512]{2,3,1,0:T(8,128)(2,1)S(1)}, u32[]{:S(2)}) copy-start(bf16[3,15,128,512]{2,3,1,0:T(8,128)(2,1)S(1)} %get-tuple-element.29) | copy-start | bytes 17694724
  267.8 8.0 %copy-start.1 = (bf16[3,15,128,512]{2,3,1,0:T(8,128)(2,1)}, bf16[3,15,128,512]{2,3,1,0:T(8,128)(2,1)S(1)}, u32[]{:S(2)}) copy-start(bf16[3,15,128,512]{2,3,1,0:T(8,128)(2,1)S(1)} %get-tuple-element.30) | copy-start | bytes 17694724
  269.0 3.1 copy-start.3
  272.1 3.6 %copy-start.2 = (f32[8,128,512]{1,2,0:T(8,128)}, f32[8,128,512]{1,2,0:T(8,128)S(1)}, u32[]{:S(2)}) copy-start(f32[8,128,512]{1,2,0:T(8,128)S(1)} %get-tuple-element.24) | copy-start | bytes 6291460
  275.8 4.2 %copy-start.4 = (f32[8,128,512]{1,2,0:T(8,128)}, f32[8,128,512]{1,2,0:T(8,128)S(1)}, u32[]{:S(2)}) copy-start(f32[8,128,512]{1,2,0:T(8,128)S(1)} %get-tuple-element.12) | copy-start | bytes 6291460
where the time goes:
time: 328 us; the launch traced here: 321 us
  waiting for transfers between devices  161 us (49%)
  matrix products  48.4 us (15%)
  starting transfers between devices  32.6 us (10%)
  blocking collectives  29 us (9%)
  other arithmetic  26.9 us (8%)
  local copies, waits for them, and re-layouts  22.7 us (7%)
    all_to_all x1, waiting for transfers between devices, shards(): lax.all_to_all(outgoing, 'sky', split_axis=0, concat_axis=0, tiled=True)  120 us
    dot_general x3, matrix products, smooth(): jnp.einsum('vy,cyz->cvz', down_matrix, across, preferred_element_type=jnp...  38.1 us
    psum x1, blocking collectives, shards(): totals = lax.psum(powers, 'sky')  29 us
    ppermute x2, waiting for transfers between devices, extended(): lax.ppermute(lax.slice_in_dim(block, block.shape[dim] - width, None, axis...  27.8 us
    ppermute x2, starting transfers between devices, extended(): lax.ppermute(lax.slice_in_dim(block, block.shape[dim] - width, None, axis...  12.7 us
    reduce_sum x4, other arithmetic, kernel_boxcars(): power = jnp.stack([jnp.sum(item * item, axis=(1, 2)) for item in found])  12 us
    max x1, other arithmetic, raise_score(): best = jnp.maximum(best, jnp.abs(running) * factor[width][:, None, None])  9.23 us
    dot_general x1, matrix products, block_values(): jnp.einsum('bs,scyx->bcyx', onehot, arrived, preferred_element_type=jnp.f...  8.3 us
  transfers between devices with their start and end apart: 7, of which 6 were waited for; matrix products, arithmetic and copies ran while one was open for 7% of the time, Pallas kernels for 0%

commit v1 on v0

v1 whole, which is shorter than its diff:
```python
import functools
import numpy as np
import ml_dtypes
import jax
import jax.numpy as jnp
from jax import lax
from jax.experimental import pallas as pl
from jax.experimental.pallas import tpu as pltpu
from jax.sharding import PartitionSpec as P

ROWB = 1
COLB = 4
BLK = 128
RIM = 8
EDGE = 7
KERNELS = 3
WIDTHS = 4
NEAR = 16
REGULARIZER = 0.05
EPSILON = 1e-06
KERNEL_FWHM = (3.0, 6.0, 9.0)
HALF_WIDTHS = (0, 1, 3, 7)
CELLS = 2048 * 512
MESH = pl.DeviceIdType.MESH
VMEM = pltpu.VMEM
F32 = jnp.float32
BF16 = jnp.bfloat16


def band_constants():
    across, down = [], []
    for fwhm in KERNEL_FWHM:
        offsets = np.arange(-RIM, RIM + 1).astype(np.float32)
        sigma = np.float32(fwhm / 2.3548)
        taps = np.exp(-offsets * offsets / (np.float32(2.0) * sigma * sigma)).astype(ml_dtypes.bfloat16)

        def pick(distance):
            inside = np.abs(distance) <= RIM
            return np.where(inside, taps[np.clip(distance + RIM, 0, 2 * RIM)], taps.dtype.type(0))

        columns = np.arange(COLB * BLK)
        across.append(pick(columns[:, None] - columns[None, :]))
        rows = np.arange(BLK)
        source = np.concatenate([rows, np.arange(-NEAR, 0), BLK + np.arange(NEAR)])
        down.append(pick(source[None, :] - rows[:, None]))
    return jnp.asarray(np.stack(across)), jnp.asarray(np.stack(down))


def box_sums(a):
    count = len(a) - 2 * EDGE
    two = {i: a[i] + a[i + 1] for i in range(4, 16)}
    three = {i: two[i] + a[i + 2] for i in range(6, 16)}
    four = {i: two[i] + two[i + 2] for i in range(4, 12)}
    own = four[7] + four[11]
    low = {6: a[6]}
    for i in range(5, -1, -1):
        low[i] = a[i] + low[i + 1]
    high = {1: a[15]}
    for i in range(2, 8):
        high[i] = high[i - 1] + a[i + 14]
    found = []
    for c in range(count):
        wide = own
        if c in low:
            wide = wide + low[c]
        if c in high:
            wide = wide + high[c]
        found.append((a[c + 7], three[c + 6], four[c + 4] + three[c + 8], wide))
    return found


def smooth_kernel(cpad_ref, across_ref, down_ref, out_ref, power_ref, acc_ref):
    k = pl.program_id(0)
    total = cpad_ref.shape[0]
    channels = total - 2 * EDGE

    def channel(c, _):
        across = jnp.dot(cpad_ref[c], across_ref[0], preferred_element_type=F32).astype(BF16)
        down = jnp.dot(down_ref[0], across, preferred_element_type=F32)
        out_ref[0, c] = down.astype(BF16)
        return 0

    lax.fori_loop(0, total, channel, 0)
    acc_ref[...] = jnp.zeros_like(acc_ref)

    def chunk(i, _):
        rows = pl.ds(pl.multiple_of((i // COLB) * NEAR, NEAR), NEAR)
        columns = pl.ds(pl.multiple_of((i % COLB) * BLK, BLK), BLK)
        a = [out_ref[0, c, rows, columns].astype(F32) for c in range(total)]
        for c, found in enumerate(box_sums(a)):
            for w, item in enumerate(found):
                square = item * item
                acc_ref[w, c] += square[:8] + square[8:]
        return 0

    lax.fori_loop(0, (BLK // NEAR) * COLB, chunk, 0)
    lane = lax.broadcasted_iota(jnp.int32, (channels, BLK), 1)

    @pl.when(k == 0)
    def _():
        power_ref[...] = jnp.zeros_like(power_ref)

    for w in range(WIDTHS):
        value = jnp.sum(jnp.sum(acc_ref[w], axis=1), axis=1, keepdims=True)
        power_ref[...] = jnp.where(lane == k * WIDTHS + w, value, power_ref[...])


def smooth_and_power(cpad):
    across, down = band_constants()
    total = cpad.shape[0]
    channels = total - 2 * EDGE
    return pl.pallas_call(
        smooth_kernel,
        grid=(KERNELS,),
        out_shape=(
            jax.ShapeDtypeStruct((KERNELS, total, BLK, COLB * BLK), BF16),
            jax.ShapeDtypeStruct((channels, BLK), F32),
        ),
        in_specs=[
            pl.BlockSpec(cpad.shape, lambda k: (0, 0, 0)),
            pl.BlockSpec((1,) + across.shape[1:], lambda k: (k, 0, 0)),
            pl.BlockSpec((1,) + down.shape[1:], lambda k: (k, 0, 0)),
        ],
        out_specs=(
            pl.BlockSpec((1, total, BLK, COLB * BLK), lambda k: (k, 0, 0, 0)),
            pl.BlockSpec((channels, BLK), lambda k: (0, 0)),
        ),
        scratch_shapes=[VMEM((WIDTHS, channels, 8, BLK), F32)],
        compiler_params=pltpu.CompilerParams(vmem_limit_bytes=40 * 2**20),
        name="smooth_and_power",
    )(cpad, across, down)


def factor_kernel(count, power_ref, clip_ref, factor_ref, arrived, send_sem, recv_sem):
    me = lax.axis_index("sky")
    barrier = pltpu.get_barrier_semaphore()

    def greet(d, _):
        pl.semaphore_signal(barrier, 1, device_id={"sky": lax.rem(me + d, count)}, device_id_type=MESH)
        return 0

    lax.fori_loop(1, count, greet, 0)
    pl.semaphore_wait(barrier, count - 1)

    def copy(d):
        return pltpu.make_async_remote_copy(
            src_ref=power_ref,
            dst_ref=arrived.at[d],
            send_sem=send_sem.at[d],
            recv_sem=recv_sem.at[d],
            device_id={"sky": lax.rem(me + d, count)},
            device_id_type=MESH,
        )

    def start(d, _):
        copy(d).start()
        return 0

    def finish(d, _):
        copy(d).wait()
        return 0

    lax.fori_loop(1, count, start, 0)
    lax.fori_loop(1, count, finish, 0)
    total = power_ref[...]
    for d in range(1, count):
        total = total + arrived[d]
    noise = jnp.sqrt(total * (1.0 / CELLS) + EPSILON)
    factor_ref[...] = 10.0 / (clip_ref[...] * noise)


def clip_factors(power, clip_tenths):
    channels = power.shape[0]
    clip = clip_tenths.astype(F32).reshape(1, KERNELS * WIDTHS)
    clip = jnp.pad(clip, ((0, 0), (0, BLK - KERNELS * WIDTHS)), constant_values=1.0)
    clip = jnp.broadcast_to(clip, (channels, BLK))
    count = lax.axis_size("sky")
    return pl.pallas_call(
        functools.partial(factor_kernel, count),
        out_shape=jax.ShapeDtypeStruct(power.shape, F32),
        in_specs=[pl.BlockSpec(memory_space=VMEM)] * 2,
        out_specs=pl.BlockSpec(memory_space=VMEM),
        scratch_shapes=[
            VMEM((count, channels, BLK), F32),
            pltpu.SemaphoreType.DMA((count,)),
            pltpu.SemaphoreType.DMA((count,)),
        ],
        compiler_params=pltpu.CompilerParams(collective_id=3, has_side_effects=True),
        name="clip_factors",
    )(power, clip)


def score_kernel(factor_ref, smoothed_ref, out_ref):
    total = smoothed_ref.shape[1]
    for column in range(COLB):
        columns = slice(column * BLK, (column + 1) * BLK)
        best = [None] * (total - 2 * EDGE)
        for k in range(KERNELS):
            a = [smoothed_ref[k, c, :, columns].astype(F32) for c in range(total)]
            for c, found in enumerate(box_sums(a)):
                for w, item in enumerate(found):
                    score = jnp.abs(item) * factor_ref[c, k * WIDTHS + w]
                    best[c] = score if best[c] is None else jnp.maximum(best[c], score)
        for c, item in enumerate(best):
            out_ref[c, :, columns] = item


def scores(factor, smoothed):
    total = smoothed.shape[1]
    channels = total - 2 * EDGE
    return pl.pallas_call(
        score_kernel,
        grid=(BLK // NEAR,),
        out_shape=jax.ShapeDtypeStruct((channels, BLK, COLB * BLK), F32),
        in_specs=[
            pl.BlockSpec(memory_space=pltpu.SMEM),
            pl.BlockSpec((KERNELS, total, NEAR, COLB * BLK), lambda i: (0, 0, i, 0)),
        ],
        out_specs=pl.BlockSpec((channels, NEAR, COLB * BLK), lambda i: (0, i, 0)),
        compiler_params=pltpu.CompilerParams(vmem_limit_bytes=40 * 2**20),
        name="scores",
    )(factor, smoothed)


def neighbours(axis):
    count = lax.axis_size(axis)
    forward = [(i, i + 1) for i in range(count - 1)]
    backward = [(target, source) for source, target in forward]
    return forward, backward


def owner_tables(beams_in, labels_in, tile_blocks):
    onehot = labels_in[None, :] == jnp.arange(tile_blocks)[:, None]
    beam_wide = beams_in.astype(F32)
    coverage = (
        jnp.einsum(
            "bs,syx->byx", onehot.astype(F32), beam_wide * beam_wide, precision=lax.Precision.HIGHEST
        )
        + REGULARIZER
    )
    return (onehot.astype(BF16), coverage)


def block_values(onehot, coverage, arrived):
    numerator = jnp.einsum("bs,scyx->bcyx", onehot, arrived, preferred_element_type=F32)
    return (numerator / coverage[:, None]).astype(BF16)


def shards(pieces, beam, destination, clip_tenths):
    sky_count = lax.axis_size("sky")
    piece_count, channels, block_size, _ = pieces.shape
    tile_blocks = ROWB * COLB
    capacity = max(2, 2 * piece_count // sky_count)
    slot_total = sky_count * capacity
    owners = destination // tile_blocks
    numbering = jnp.arange(piece_count)
    earlier = (owners[None, :] == owners[:, None]) & (numbering[None, :] < numbering[:, None])
    position = jnp.sum(earlier.astype(jnp.int32), axis=1)
    slot_index = owners * capacity + position
    weighted = (beam[:, None].astype(F32) * pieces.astype(F32)).astype(BF16)
    outgoing = jnp.zeros((slot_total, channels, block_size, block_size), BF16).at[slot_index].set(weighted)
    beams_out = jnp.zeros((slot_total, block_size, block_size), BF16).at[slot_index].set(beam)
    labels_out = jnp.full((slot_total,), -1, jnp.int32).at[slot_index].set(destination % tile_blocks)
    arrived, beams_in, labels_in = (
        lax.all_to_all(outgoing, "sky", split_axis=0, concat_axis=0, tiled=True),
        lax.all_to_all(beams_out, "sky", split_axis=0, concat_axis=0, tiled=True),
        lax.all_to_all(labels_out, "sky", split_axis=0, concat_axis=0, tiled=True),
    )
    onehot, coverage = owner_tables(beams_in, labels_in, tile_blocks)
    tile_values = block_values(onehot, coverage, arrived)
    combined = tile_values.reshape(ROWB, COLB, channels, block_size, block_size).transpose(2, 0, 3, 1, 4)
    combined = combined.reshape(channels, ROWB * block_size, COLB * block_size)
    forward, backward = neighbours("sky")
    above = lax.ppermute(combined[:, -NEAR:], "sky", forward)
    below = lax.ppermute(combined[:, :NEAR], "sky", backward)
    tall = jnp.concatenate([combined, above, below], axis=1)
    forward, backward = neighbours("freq")
    low = lax.ppermute(tall[-EDGE:], "freq", forward)
    high = lax.ppermute(tall[:EDGE], "freq", backward)
    cpad = jnp.concatenate([low, tall, high], axis=0)
    smoothed, power = smooth_and_power(cpad)
    factor = clip_factors(power, clip_tenths)
    return scores(factor, smoothed)


def solution(mesh):
    return jax.shard_map(
        shards,
        mesh=mesh,
        in_specs=(P("sky", "freq", None, None), P("sky", None, None), P("sky"), P()),
        out_specs=P("freq", "sky", None),
        check_vma=False,
    )
```

time: 328 us -> 275 us (0.84); the launches traced: 321 us -> 272 us
  Pallas kernels: 0 us -> 49.8 us
  matrix products: 48.4 us -> 10.3 us
  blocking collectives: 29 us -> 0 us
  other arithmetic: 26.9 us -> 5.52 us
  waiting for transfers between devices: 161 us -> 148 us
  local copies, waits for them, and re-layouts: 22.7 us -> 26.8 us
    pallas_call x0 -> x3, Pallas kernels: none -> 49.8 us  [the longest x1 32.4 us: smooth_and_power(): pl.pallas_call(smooth_kernel, grid=(KERNELS,), out_shape=(jax.ShapeDtypeS...]
    dot_general x5 -> x2, matrix products: 48.4 us -> 10.3 us  [the longest x1 8.3 us: block_values(): jnp.einsum('bs,scyx->bcyx', onehot, arrived, preferred_element_type=F32)]
    psum x1 -> x0, blocking collectives: 29 us -> none  [shards(): totals = lax.psum(powers, 'sky')]
    ppermute x4, waiting for transfers between devices: 35.6 us -> 19.8 us  [the longest x1 11 us: shards(): low = lax.ppermute(tall[-EDGE:], 'freq', forward)]
    reduce_sum x4 -> x0, other arithmetic: 12 us -> none  [kernel_boxcars(): power = jnp.stack([jnp.sum(item * item, axis=(1, 2)) for item in found])]
    max x1 -> x0, other arithmetic: 9.23 us -> none  [raise_score(): best = jnp.maximum(best, jnp.abs(running) * factor[width][:, None, None])]
    unnamed x18, local copies, waits for them, and re-layouts: 0.13 us -> 8.17 us
    broadcast_in_dim x2 -> x4, local copies, waits for them, and re-layouts: 6.54 us -> 7.18 us  [the longest x1 5.37 us: shards(): jnp.zeros((slot_total, channels, block_size, block_size), BF16)]
  transfers between devices with their start and end apart: 7 -> 7, of which waited for: 6 -> 7; matrix products, arithmetic and copies ran while one was open for 7% -> 7% of each run, Pallas kernels for 0% -> 0%
where the time goes in v1:
time: 275 us; the launch traced here: 272 us
  waiting for transfers between devices  148 us (54%)
  Pallas kernels  49.8 us (18%)
  starting transfers between devices  32.1 us (12%)
  local copies, waits for them, and re-layouts  26.8 us (10%)
  matrix products  10.3 us (4%)
  other arithmetic  5.52 us (2%)
    all_to_all x1, waiting for transfers between devices, shards(): lax.all_to_all(outgoing, 'sky', split_axis=0, concat_axis=0, tiled=True)  123 us
    pallas_call x1, Pallas kernels, smooth_and_power(): pl.pallas_call(smooth_kernel, grid=(KERNELS,), out_shape=(jax.ShapeDtypeS...  32.4 us
    ppermute x1, starting transfers between devices, shards(): low = lax.ppermute(tall[-EDGE:], 'freq', forward)  11.4 us
    ppermute x1, waiting for transfers between devices, shards(): low = lax.ppermute(tall[-EDGE:], 'freq', forward)  11 us
    pallas_call x1, Pallas kernels, clip_factors(): pl.pallas_call(functools.partial(factor_kernel, count), out_shape=jax.Sha...  9.93 us
    dot_general x1, matrix products, block_values(): jnp.einsum('bs,scyx->bcyx', onehot, arrived, preferred_element_type=F32)  8.3 us
    unnamed x18, local copies, waits for them, and re-layouts  8.17 us
    all_to_all x1, starting transfers between devices, shards(): lax.all_to_all(labels_out, 'sky', split_axis=0, concat_axis=0, tiled=True)  7.58 us
  transfers between devices with their start and end apart: 7, of which 7 were waited for; matrix products, arithmetic and copies ran while one was open for 7% of the time, Pallas kernels for 0%

profile of v1, /device:TPU:1, one launch (start us, length us, event | category | flops | bytes accessed | tf_op | source)
XLA Modules:
  0.0 272.3 jit_solution(15114554778602772400)
XLA Ops:
  2.2 7.6 %all-to-all-start = ((s32[16,2,1]{1,2,0:T(1,128)}), s32[16,2,1]{1,2,0:T(1,128)S(1)}, u32[]{:S(2)}, u32[]{:S(2)}) async-start(s32[16,2,1]{1,2,0:T(1,128)} %bitcast), calls=%async_computation | async-start | bytes 16384 | tf_op jit(solution)/shard_map/all_to_all | solution.py:267
  11.0 2.4 scatter_fusion.1
  13.4 2.8 %all-to-all-done = s32[16,2,1]{1,2,0:T(1,128)S(1)} async-done(((s32[16,2,1]{1,2,0:T(1,128)}), s32[16,2,1]{1,2,0:T(1,128)S(1)}, u32[]{:S(2)}, u32[]{:S(2)}) %all-to-all-start) | async-done | bytes 160 | tf_op jit(solution)/shard_map/all_to_all | solution.py:267
  16.2 3.9 %all-to-all-start.2 = ((bf16[32,128,128]{2,1,0:T(8,128)(2,1)}), bf16[32,128,128]{2,1,0:T(8,128)(2,1)S(1)}, u32[]{:S(2)}, u32[]{:S(2)}) async-start(bf16[32,128,128]{2,1,0:T(8,128)(2,1)} %scatter_fusion.1), calls=%async_computation.2 | async-start | bytes 2097152 | tf_op jit(solution)/shard_map/all_to_all | solution.py:266
  20.1 2.2 multiply_convert_fusion
  22.3 5.4 %broadcast_in_dim.14 = bf16[32,8,128,128]{3,2,1,0:T(8,128)(2,1)} broadcast(bf16[]{:T(256)} %constant.42.clone.1), dimensions={} | broadcast | bytes 8388610 | tf_op jit(solution)/shard_map/broadcast_in_dim | solution.py:261
  27.7 5.0 %scatter_fusion = bf16[32,8,128,128]{3,2,1,0:T(8,128)(2,1)} fusion(bf16[32,8,128,128]{3,2,1,0:T(8,128)(2,1)} %broadcast_in_dim.14, s32[8]{0:T(128)S(1)} %compare_select_fusion, bf16[8,8,128,128]{3,2,1,0:T(8,128)(2,1)S(1)} %multiply_convert_fusion), kind=kCustom, calls=%fused_computation.1 | custom fusion | bytes 6291488 | tf_op jit(solution)/shard_map/scatter | solution.py:261
  32.7 2.4 all-to-all-done.2
  35.1 4.7 %all-to-all-start.1 = ((bf16[32,8,128,128]{3,2,1,0:T(8,128)(2,1)}), bf16[32,8,128,128]{3,2,1,0:T(8,128)(2,1)}, u32[]{:S(2)}, u32[]{:S(2)}) async-start(bf16[32,8,128,128]{3,2,1,0:T(8,128)(2,1)} %scatter_fusion), calls=%async_computation.1 | async-start | bytes 16777216 | tf_op jit(solution)/shard_map/all_to_all | solution.py:265
  41.4 2.0 fusion.4
  43.3 122.6 %all-to-all-done.1 = bf16[32,8,128,128]{3,2,1,0:T(8,128)(2,1)} async-done(((bf16[32,8,128,128]{3,2,1,0:T(8,128)(2,1)}), bf16[32,8,128,128]{3,2,1,0:T(8,128)(2,1)}, u32[]{:S(2)}, u32[]{:S(2)}) %all-to-all-start.1) | async-done | bytes 8388640 | tf_op jit(solution)/shard_map/all_to_all | solution.py:265
  166.0 8.3 %fusion.7 = bf16[8,1,128,4,128]{4,3,2,0,1:T(4,128)(2,1)S(1)} fusion(f32[4,128,128]{2,0,1:T(4,128)S(1)} %fusion.4, bf16[32,8,128,128]{3,2,1,0:T(8,128)(2,1)} %all-to-all-done.1, s32[32]{0:T(128)S(1)} %eq.33), kind=kOutput, calls=%fused_computation.12 | convolution fusion | flops 34603136 | bytes 9699456 | tf_op jit(solution)/shard_map/bs,scyx->bcyx/dot_general | solution.py:245
  178.0 3.8 %collective-permute-done.1 = bf16[8,16,512]{2,1,0:T(8,128)(2,1)S(1)} collective-permute-done((bf16[8,16,512]{2,1,0:T(8,128)(2,1)S(1)}, bf16[8,16,512]{2,1,0:T(8,128)(2,1)S(1)}, u32[]{:S(2)}, u32[]{:S(2)}) %collective-permute-start.1) | collective-permute-done | bytes 131104 | tf_op jit(solution)/shard_map/ppermute | solution.py:275
  181.8 1.6 fusion.19
  183.4 11.4 %collective-permute-start.2 = (bf16[7,160,512]{2,1,0:T(8,128)(2,1)}, bf16[7,160,512]{2,1,0:T(8,128)(2,1)S(1)}, u32[]{:S(2)}, u32[]{:S(2)}) collective-permute-start(bf16[7,160,512]{2,1,0:T(8,128)(2,1)} %get-tuple-element.9), channel_id=1, source_target_pairs={{0,1},{1,2},{2,3},{3,4},{4,5},{5,6},{6,7},{7,8},{8,9},{9,10},{10,1... | collective-permute-start | bytes 3440648 | tf_op jit(solution)/shard_map/ppermute | solution.py:278
  194.8 1.9 collective-permute-start.3
  196.9 11.0 %collective-permute-done.2 = bf16[7,160,512]{2,1,0:T(8,128)(2,1)S(1)} collective-permute-done((bf16[7,160,512]{2,1,0:T(8,128)(2,1)}, bf16[7,160,512]{2,1,0:T(8,128)(2,1)S(1)}, u32[]{:S(2)}, u32[]{:S(2)}) %collective-permute-start.2) | collective-permute-done | bytes 1146912 | tf_op jit(solution)/shard_map/ppermute | solution.py:278
  207.9 4.4 %collective-permute-done.3 = bf16[7,160,512]{2,1,0:T(8,128)(2,1)} collective-permute-done((bf16[7,160,512]{2,1,0:T(8,128)(2,1)}, bf16[7,160,512]{2,1,0:T(8,128)(2,1)}, u32[]{:S(2)}, u32[]{:S(2)}) %collective-permute-start.3) | collective-permute-done | bytes 1146912 | tf_op jit(solution)/shard_map/ppermute | solution.py:279
  212.3 1.5 pad_maximum_fusion.cpad_ref
  213.8 32.4 %smooth_and_power.1 = (bf16[3,22,128,512]{3,2,1,0:T(8,128)(2,1)S(1)}, f32[8,128]{1,0:T(8,128)S(1)}) custom-call(bf16[22,160,512]{2,1,0:T(8,128)(2,1)S(1)} %pad_maximum_fusion.cpad_ref, bf16[3,512,512]{2,1,0:T(8,128)(2,1)S(1)} %copy-done.2, bf16[3,128,160]{2,1,0:T(8,128)(2,1)S(1)} %copy-done.3), custom_call_target="tpu_custom_call" | custom-call | tf_op jit(solution)/shard_map/smooth_and_power/pallas_call | solution.py:112
  246.3 3.4 %copy-done = bf16[3,22,128,512]{3,2,1,0:T(8,128)(2,1)} copy-done((bf16[3,22,128,512]{3,2,1,0:T(8,128)(2,1)}, bf16[3,22,128,512]{3,2,1,0:T(8,128)(2,1)S(1)}, u32[]{:S(2)}) %copy-start) | copy-done | bytes 8650776
  250.8 9.9 %clip_factors.1.factor_ref = f32[8,128]{1,0:T(8,128)} custom-call(f32[8,128]{1,0:T(8,128)} %copy-done.5, f32[8,128]{1,0:T(8,128)} %broadcast_in_dim.34.clip_ref), custom_call_target="tpu_custom_call" | custom-call | tf_op jit(solution)/shard_map/clip_factors/pallas_call | solution.py:178
  260.8 3.4 %copy-done.1 = bf16[3,22,128,512]{3,2,1,0:T(8,128)(2,1)S(1)} copy-done((bf16[3,22,128,512]{3,2,1,0:T(8,128)(2,1)S(1)}, bf16[3,22,128,512]{3,2,1,0:T(8,128)(2,1)}, u32[]{:S(2)}) %copy-start.1) | copy-done | bytes 8650776
  264.9 7.4 %scores.1 = f32[8,128,512]{2,1,0:T(8,128)} custom-call(f32[8,128]{1,0:T(8,128)S(1)} %copy-done.4, bf16[3,22,128,512]{3,2,1,0:T(8,128)(2,1)S(1)} %copy-done.1), custom_call_target="tpu_custom_call" | custom-call | tf_op jit(solution)/shard_map/scores/pallas_call | solution.py:211
  (37 shorter events, 10.6 us)
Async XLA Ops:
  0.0 20.1 %copy-start.6 = (bf16[8,128,128]{2,1,0:T(8,128)(2,1)S(1)}, bf16[8,128,128]{2,1,0:T(8,128)(2,1)}, u32[]{:S(2)}) copy-start(bf16[8,128,128]{2,1,0:T(8,128)(2,1)} %param.7) | copy-start | bytes 786436
  2.2 14.0 %all-to-all-start = ((s32[16,2,1]{1,2,0:T(1,128)}), s32[16,2,1]{1,2,0:T(1,128)S(1)}, u32[]{:S(2)}, u32[]{:S(2)}) async-start(s32[16,2,1]{1,2,0:T(1,128)} %bitcast), calls=%async_computation | async-start | bytes 16384 | tf_op jit(solution)/shard_map/all_to_all | solution.py:267
  16.2 18.9 %all-to-all-start.2 = ((bf16[32,128,128]{2,1,0:T(8,128)(2,1)}), bf16[32,128,128]{2,1,0:T(8,128)(2,1)S(1)}, u32[]{:S(2)}, u32[]{:S(2)}) async-start(bf16[32,128,128]{2,1,0:T(8,128)(2,1)} %scatter_fusion.1), calls=%async_computation.2 | async-start | bytes 2097152 | tf_op jit(solution)/shard_map/all_to_all | solution.py:266
  35.1 130.9 %all-to-all-start.1 = ((bf16[32,8,128,128]{3,2,1,0:T(8,128)(2,1)}), bf16[32,8,128,128]{3,2,1,0:T(8,128)(2,1)}, u32[]{:S(2)}, u32[]{:S(2)}) async-start(bf16[32,8,128,128]{3,2,1,0:T(8,128)(2,1)} %scatter_fusion), calls=%async_computation.1 | async-start | bytes 16777216 | tf_op jit(solution)/shard_map/all_to_all | solution.py:265
  174.8 3.2 %collective-permute-start = (bf16[8,16,512]{2,1,0:T(8,128)(2,1)S(1)}, bf16[8,16,512]{2,1,0:T(8,128)(2,1)S(1)}, u32[]{:S(2)}, u32[]{:S(2)}) collective-permute-start(bf16[8,16,512]{2,1,0:T(8,128)(2,1)S(1)} %get-tuple-element.12), channel_id=1, source_target_pairs={{0,16},{16,32},{32,48},{48,64},{64,80},{80,96},{96,112},{112,128},... | collective-permute-start | bytes 393224 | tf_op jit(solution)/shard_map/ppermute | solution.py:274
  176.1 5.7 %collective-permute-start.1 = (bf16[8,16,512]{2,1,0:T(8,128)(2,1)S(1)}, bf16[8,16,512]{2,1,0:T(8,128)(2,1)S(1)}, u32[]{:S(2)}, u32[]{:S(2)}) collective-permute-start(bf16[8,16,512]{2,1,0:T(8,128)(2,1)S(1)} %get-tuple-element.11), channel_id=1, source_target_pairs={{16,0},{32,16},{48,32},{64,48},{80,64},{96,80},{112,96},{128,112},... | collective-permute-start | bytes 393224 | tf_op jit(solution)/shard_map/ppermute | solution.py:275
  181.8 15.0 %copy-start.7 = (s32[3,4]{1,0:T(4,128)S(1)}, s32[3,4]{1,0:T(4,128)}, u32[]{:S(2)}) copy-start(s32[3,4]{1,0:T(4,128)} %param.9) | copy-start | bytes 148
  183.4 24.5 %collective-permute-start.2 = (bf16[7,160,512]{2,1,0:T(8,128)(2,1)}, bf16[7,160,512]{2,1,0:T(8,128)(2,1)S(1)}, u32[]{:S(2)}, u32[]{:S(2)}) collective-permute-start(bf16[7,160,512]{2,1,0:T(8,128)(2,1)} %get-tuple-element.9), channel_id=1, source_target_pairs={{0,1},{1,2},{2,3},{3,4},{4,5},{5,6},{6,7},{7,8},{8,9},{9,10},{10,1... | collective-permute-start | bytes 3440648 | tf_op jit(solution)/shard_map/ppermute | solution.py:278
  194.8 17.5 %collective-permute-start.3 = (bf16[7,160,512]{2,1,0:T(8,128)(2,1)}, bf16[7,160,512]{2,1,0:T(8,128)(2,1)}, u32[]{:S(2)}, u32[]{:S(2)}) collective-permute-start(bf16[7,160,512]{2,1,0:T(8,128)(2,1)} %get-tuple-element.10), channel_id=1, source_target_pairs={{1,0},{2,1},{3,2},{4,3},{5,4},{6,5},{7,6},{8,7},{9,8},{10,9},{11,1... | collective-permute-start | bytes 3440648 | tf_op jit(solution)/shard_map/ppermute | solution.py:279
  196.8 16.9 %copy-start.2 = (bf16[3,512,512]{2,1,0:T(8,128)(2,1)S(1)}, bf16[3,512,512]{2,1,0:T(8,128)(2,1)}, u32[]{:S(2)}) copy-start(bf16[3,512,512]{2,1,0:T(8,128)(2,1)} %constant.45.clone.across_ref) | copy-start | bytes 4718596
  196.9 17.0 %copy-start.3 = (bf16[3,128,160]{2,1,0:T(8,128)(2,1)S(1)}, bf16[3,128,160]{2,1,0:T(8,128)(2,1)}, u32[]{:S(2)}) copy-start(bf16[3,128,160]{2,1,0:T(8,128)(2,1)} %constant.46.clone.down_ref) | copy-start | bytes 368644
  246.3 3.4 %copy-start = (bf16[3,22,128,512]{3,2,1,0:T(8,128)(2,1)}, bf16[3,22,128,512]{3,2,1,0:T(8,128)(2,1)S(1)}, u32[]{:S(2)}) copy-start(bf16[3,22,128,512]{3,2,1,0:T(8,128)(2,1)S(1)} %get-tuple-element.8.smoothed_ref) | copy-start | bytes 25952260
  249.6 0.6 copy-start.5
  260.8 3.5 %copy-start.1 = (bf16[3,22,128,512]{3,2,1,0:T(8,128)(2,1)S(1)}, bf16[3,22,128,512]{3,2,1,0:T(8,128)(2,1)}, u32[]{:S(2)}) copy-start(bf16[3,22,128,512]{3,2,1,0:T(8,128)(2,1)} %copy-done) | copy-start | bytes 25952260
  264.2 0.7 copy-start.4

commit v2 on v1

--- a/solution.py
+++ b/solution.py
@@ -71,11 +71,11 @@
 
 def smooth_kernel(cpad_ref, across_ref, down_ref, out_ref, power_ref, acc_ref):
     k = pl.program_id(0)
-    total = cpad_ref.shape[0]
+    total = cpad_ref.shape[0] - 2
     channels = total - 2 * EDGE
 
     def channel(c, _):
-        across = jnp.dot(cpad_ref[c], across_ref[0], preferred_element_type=F32).astype(BF16)
+        across = jnp.dot(cpad_ref[c + 1], across_ref[0], preferred_element_type=F32).astype(BF16)
         down = jnp.dot(down_ref[0], across, preferred_element_type=F32)
         out_ref[0, c] = down.astype(BF16)
         return 0
@@ -107,7 +107,7 @@
 
 def smooth_and_power(cpad):
     across, down = band_constants()
-    total = cpad.shape[0]
+    total = cpad.shape[0] - 2
     channels = total - 2 * EDGE
     return pl.pallas_call(
         smooth_kernel,
@@ -222,62 +222,387 @@
     )(factor, smoothed)
 
 
-def neighbours(axis):
-    count = lax.axis_size(axis)
-    forward = [(i, i + 1) for i in range(count - 1)]
-    backward = [(target, source) for source, target in forward]
-    return forward, backward
-
-
-def owner_tables(beams_in, labels_in, tile_blocks):
-    onehot = labels_in[None, :] == jnp.arange(tile_blocks)[:, None]
-    beam_wide = beams_in.astype(F32)
-    coverage = (
-        jnp.einsum(
-            "bs,syx->byx", onehot.astype(F32), beam_wide * beam_wide, precision=lax.Precision.HIGHEST
-        )
-        + REGULARIZER
-    )
-    return (onehot.astype(BF16), coverage)
-
-
-def block_values(onehot, coverage, arrived):
-    numerator = jnp.einsum("bs,scyx->bcyx", onehot, arrived, preferred_element_type=F32)
-    return (numerator / coverage[:, None]).astype(BF16)
+SIDE = 4
+GROUP = 4
+PIECES = 8
+STEPS = ((0, 1), (0, -1), (1, 0), (-1, 0), (1, 1), (1, -1), (-1, 1), (-1, -1))
+HALF = COLB // 2
+
+
+def combine_kernel(
+    sky_count, freq_count, pieces_ref, beam_ref, label_ref, cpad_ref,
+    held, first_out, first_in, second_out, second_in, label_all, label_s,
+    cover_out, cover_in, inverse,
+    label_sems, label_local, cover_sems, inverse_sems, wave_sems, hop_sems, first_sems, second_sems,
+    edge_send, edge_recv,
+):
+    t, f = lax.axis_index("sky"), lax.axis_index("freq")
+    x, y = t // SIDE, lax.rem(t, SIDE)
+    barrier = pltpu.get_barrier_semaphore()
+
+    def at(o, d):
+        if o == 0:
+            return lax.rem(x + d + SIDE, SIDE) * SIDE + y
+        return x * SIDE + lax.rem(y + d + SIDE, SIDE)
+
+    def remote(source, target, send, recv, sky, freq):
+        return pltpu.make_async_remote_copy(
+            src_ref=source, dst_ref=target, send_sem=send, recv_sem=recv,
+            device_id=(sky, freq), device_id_type=MESH,
+        )
+
+    def within(dt, df):
+        good = None
+        for value, delta, count in ((t, dt, sky_count), (f, df, freq_count)):
+            if delta:
+                here = value + delta
+                one = (here >= 0) & (here < count)
+                good = one if good is None else good & one
+        return good
+
+    def greet_sky(d, _):
+        pl.semaphore_signal(barrier, 1, device_id=(lax.rem(t + d, sky_count), f), device_id_type=MESH)
+        return 0
+
+    def greet_freq(d, _):
+        pl.semaphore_signal(barrier, 1, device_id=(t, lax.rem(f + d, freq_count)), device_id_type=MESH)
+        return 0
+
+    lax.fori_loop(1, sky_count, greet_sky, 0)
+    lax.fori_loop(1, freq_count, greet_freq, 0)
+    for dt, df in STEPS[4:]:
+        @pl.when(within(dt, df))
+        def _():
+            pl.semaphore_signal(barrier, 1, device_id=(t + dt, f + df), device_id_type=MESH)
+
+    def weigh(c, _):
+        for p in range(PIECES):
+            value = beam_ref[p].astype(F32) * pieces_ref[p, c].astype(F32)
+            held[c, 0, p] = value.astype(BF16)
+        return 0
+
+    lax.fori_loop(0, 2 * GROUP, weigh, 0)
+
+    total = cpad_ref.shape[0]
+    for edge, rows in ((t == 0, pl.ds(BLK, NEAR)), (t == sky_count - 1, pl.ds(BLK + NEAR, NEAR))):
+        @pl.when(edge)
+        def _():
+            def clear(c, _):
+                cpad_ref[c, rows, :] = jnp.zeros((NEAR, COLB * BLK), BF16)
+                return 0
+            lax.fori_loop(0, total, clear, 0)
+    for edge, start in ((f == 0, 0), (f == freq_count - 1, 4 * GROUP)):
+        @pl.when(edge)
+        def _():
+            def clear(c, _):
+                cpad_ref[start + c] = jnp.zeros(cpad_ref.shape[1:], BF16)
+                return 0
+            lax.fori_loop(0, 2 * GROUP, clear, 0)
+
+    diagonals = jnp.int32(0)
+    for dt, df in STEPS[4:]:
+        diagonals = diagonals + within(dt, df).astype(jnp.int32)
+    pl.semaphore_wait(barrier, sky_count - 1 + freq_count - 1 + diagonals)
+
+    def wave(o, i, side):
+        c = o * GROUP + i
+        return remote(
+            held.at[c, 0], held.at[c, 1 if side == 1 else 3],
+            wave_sems.at[0, c, (1 - side) // 2], wave_sems.at[1, c, (1 - side) // 2], at(o, side), f,
+        )
+
+    def onward(o, i, side):
+        c = o * GROUP + i
+        half = pl.ds(0 if side == 1 else PIECES // 2, PIECES // 2)
+        return remote(
+            held.at[c, 1 if side == 1 else 3, half], held.at[c, 2, half],
+            hop_sems.at[0, c, (1 - side) // 2], hop_sems.at[1, c, (1 - side) // 2], at(o, side), f,
+        )
+
+    def first(o, i, side):
+        c = o * GROUP + i
+        n = (1 - side) // 2
+        return remote(
+            first_out.at[c, n], first_in.at[c, n], first_sems.at[0, c, n], first_sems.at[1, c, n], at(1 - o, side), f
+        )
+
+    def second(o, i, side):
+        c = o * GROUP + i
+        n = (1 - side) // 2
+        return remote(
+            second_out.at[c, n], second_in.at[c, n], second_sems.at[0, c, n], second_sems.at[1, c, n],
+            at(1 - o, side), f,
+        )
+
+    SIDES = (1, -1)
+    ORIENTATIONS = (0, 1)
+
+    def label_copy(d):
+        return remote(
+            label_ref, label_all.at[t], label_sems.at[0, d], label_sems.at[1, d], lax.rem(t + d, sky_count), f
+        )
+
+    def start_labels(d, _):
+        label_copy(d).start()
+        return 0
+
+    lax.fori_loop(1, sky_count, start_labels, 0)
+    for o in ORIENTATIONS:
+        for side in SIDES:
+            wave(o, 0, side).start()
+
+    pair = pl.ds(pl.multiple_of((f // 2) * NEAR, NEAR), NEAR)
+    squares = []
+    for p in range(PIECES):
+        both = beam_ref[p, pair, :].astype(F32)
+        mine = jnp.where(lax.rem(f, 2) == 0, both[:8], both[8:])
+        squares.append(mine * mine)
+    labels = [jnp.broadcast_to(label_ref[p : p + 1, :], (8, BLK)) for p in range(PIECES)]
+
+    def cover(tile, _):
+        for b in range(COLB):
+            found = jnp.zeros((8, BLK), F32)
+            for p in range(PIECES):
+                found = found + jnp.where(labels[p] == tile * COLB + b, squares[p], 0.0)
+            cover_out[tile, b] = found
+        return 0
+
+    lax.fori_loop(0, sky_count, cover, 0)
+
+    def cover_copy(d):
+        other = lax.rem(t + d, sky_count)
+        return remote(cover_out.at[other], cover_in.at[d], cover_sems.at[0, d], cover_sems.at[1, d], other, f)
+
+    def start_cover(d, _):
+        cover_copy(d).start()
+        return 0
+
+    lax.fori_loop(1, sky_count, start_cover, 0)
+    for o in ORIENTATIONS:
+        for side in SIDES:
+            wave(o, 1, side).start()
+
+    def finish_labels(d, _):
+        label_copy(d).wait_send()
+        source = lax.rem(t - d + sky_count, sky_count)
+        remote(
+            label_ref, label_all.at[source], label_sems.at[0, d], label_sems.at[1, d], source, f
+        ).wait_recv()
+        return 0
+
+    label_all[t] = label_ref[...]
+    lax.fori_loop(1, sky_count, finish_labels, 0)
+    to_scalars = pltpu.make_async_copy(label_all, label_s, label_local)
+    to_scalars.start()
+
+    def finish_cover(d, _):
+        cover_copy(d).wait()
+        return 0
+
+    lax.fori_loop(1, sky_count, finish_cover, 0)
+    coverage = cover_out[t] + REGULARIZER
+    for d in range(1, sky_count):
+        coverage = coverage + cover_in[d]
+    inverse[f] = 1.0 / coverage
+
+    def inverse_copy(d):
+        return remote(
+            inverse.at[f], inverse.at[f], inverse_sems.at[0, d], inverse_sems.at[1, d],
+            t, lax.rem(f + d, freq_count),
+        )
+
+    def start_inverse(d, _):
+        inverse_copy(d).start()
+        return 0
+
+    lax.fori_loop(1, freq_count, start_inverse, 0)
+    to_scalars.wait()
+
+    def finish_inverse(d, _):
+        inverse_copy(d).wait_send()
+        source = lax.rem(f - d + freq_count, freq_count)
+        remote(
+            inverse.at[source], inverse.at[source], inverse_sems.at[0, d], inverse_sems.at[1, d], t, source
+        ).wait_recv()
+        return 0
+
+    ROWS = 64
+
+    def sums(o, c, d, blocks, rows):
+        base = at(1 - o, d) * COLB
+
+        def source(j, found):
+            sky = at(o, -j)
+            found = list(found)
+            for p in range(PIECES):
+                value = held[c, j, p, rows, :].astype(F32)
+                label = label_s[sky, p, 0]
+                for n, b in enumerate(blocks):
+                    found[n] = found[n] + jnp.where(label == base + b, 1.0, 0.0) * value
+            return tuple(found)
+
+        return lax.fori_loop(0, SIDE, source, tuple(jnp.zeros((ROWS, BLK), F32) for _ in blocks))
+
+    def by_rows(body):
+        def chunk(r, _):
+            body(pl.ds(pl.multiple_of(r * ROWS, ROWS), ROWS), r)
+            return 0
+        lax.fori_loop(0, BLK // ROWS, chunk, 0)
+
+    def edge_copy(c, n):
+        dt, df = STEPS[n]
+        rows = {0: pl.ds(0, BLK), 1: pl.ds(BLK - NEAR, NEAR), -1: pl.ds(0, NEAR)}[dt]
+        land = {0: pl.ds(0, BLK), 1: pl.ds(BLK, NEAR), -1: pl.ds(BLK + NEAR, NEAR)}[dt]
+        own = 2 * GROUP + c
+        return remote(
+            cpad_ref.at[own, rows], cpad_ref.at[own - 2 * GROUP * df, land],
+            edge_send.at[n, c], edge_recv.at[n, c], t + dt, f + df,
+        )
+
+    def step(n, _):
+        @pl.when(n < GROUP)
+        def _():
+            for o in ORIENTATIONS:
+                for side in SIDES:
+                    wave(o, n, side).wait_recv()
+                    onward(o, n, side).start()
+
+        @pl.when(n < GROUP - 2)
+        def _():
+            for o in ORIENTATIONS:
+                for side in SIDES:
+                    wave(o, n + 2, side).start()
+
+        @pl.when((n >= 1) & (n < GROUP + 1))
+        def _():
+            i = n - 1
+            for o in ORIENTATIONS:
+                c = o * GROUP + i
+                for side in SIDES:
+                    onward(o, i, side).wait_recv()
+
+                def far(rows, r):
+                    found = sums(o, c, 2, tuple(range(COLB)), rows)
+                    for b in range(COLB):
+                        first_out[c, b // HALF, b % HALF, rows, :] = found[b].astype(BF16)
+
+                by_rows(far)
+                for side in SIDES:
+                    first(o, i, side).start()
+
+        @pl.when((n >= 2) & (n < GROUP + 2))
+        def _():
+            i = n - 2
+            for o in ORIENTATIONS:
+                c = o * GROUP + i
+                for m, side in enumerate(SIDES):
+                    first(o, i, side).wait_recv()
+
+                    def near(rows, r):
+                        found = list(sums(o, c, side, tuple(range(COLB)), rows))
+                        for b in range(HALF):
+                            found[m * HALF + b] = found[m * HALF + b] + first_in[c, m, b, rows, :].astype(F32)
+                        for b in range(COLB):
+                            second_out[c, m, b, rows, :] = found[b].astype(BF16)
+
+                    by_rows(near)
+                    second(o, i, side).start()
+
+        @pl.when(n == 3)
+        def _():
+            lax.fori_loop(1, freq_count, finish_inverse, 0)
+
+        @pl.when(n >= 3)
+        def _():
+            i = n - 3
+            for o in ORIENTATIONS:
+                c = o * GROUP + i
+                for side in SIDES:
+                    second(o, i, side).wait_recv()
+
+                def own(rows, r):
+                    found = sums(o, c, 0, tuple(range(COLB)), rows)
+                    for b in range(COLB):
+                        value = found[b]
+                        for m in range(2):
+                            value = value + second_in[c, m, b, rows, :].astype(F32)
+                        scale = jnp.concatenate([inverse[r * (ROWS // 8) + q, b] for q in range(ROWS // 8)], axis=0)
+                        cpad_ref[2 * GROUP + c, rows, b * BLK : (b + 1) * BLK] = (value * scale).astype(BF16)
+
+                by_rows(own)
+                for m, (dt, df) in enumerate(STEPS):
+                    @pl.when(within(dt, df))
+                    def _():
+                        edge_copy(c, m).start()
+        return 0
+
+    lax.fori_loop(0, GROUP + 3, step, 0)
+
+    def finish(c, _):
+        for m, (dt, df) in enumerate(STEPS):
+            @pl.when(within(-dt, -df))
+            def _():
+                edge_copy(c, m).wait_recv()
+
+            @pl.when(within(dt, df))
+            def _():
+                edge_copy(c, m).wait_send()
+        return 0
+
+    lax.fori_loop(0, 2 * GROUP, finish, 0)
+
+    def drain(i, _):
+        for o in ORIENTATIONS:
+            for side in SIDES:
+                for copy in (wave, onward, first, second):
+                    copy(o, i, side).wait_send()
+        return 0
+
+    lax.fori_loop(0, GROUP, drain, 0)
+
+
+def combine(pieces, beam, destination):
+    sky_count, freq_count = lax.axis_size("sky"), lax.axis_size("freq")
+    piece_count, channels = pieces.shape[:2]
+    labels = jnp.broadcast_to(destination[:, None], (piece_count, BLK))
+    dma = pltpu.SemaphoreType.DMA
+    plane = (BLK, BLK)
+    return pl.pallas_call(
+        functools.partial(combine_kernel, sky_count, freq_count),
+        out_shape=jax.ShapeDtypeStruct((3 * channels, BLK + 2 * NEAR, COLB * BLK), BF16),
+        in_specs=[pl.BlockSpec(memory_space=VMEM)] * 3,
+        out_specs=pl.BlockSpec(memory_space=VMEM),
+        scratch_shapes=[
+            VMEM((channels, SIDE, piece_count) + plane, BF16),
+            VMEM((channels, 2, HALF) + plane, BF16),
+            VMEM((channels, 2, HALF) + plane, BF16),
+            VMEM((channels, 2, COLB) + plane, BF16),
+            VMEM((channels, 2, COLB) + plane, BF16),
+            VMEM((sky_count, piece_count, BLK), jnp.int32),
+            pltpu.SMEM((sky_count, piece_count, BLK), jnp.int32),
+            VMEM((sky_count, COLB, 8, BLK), F32),
+            VMEM((sky_count, COLB, 8, BLK), F32),
+            VMEM((freq_count, COLB, 8, BLK), F32),
+            dma((2, sky_count)),
+            dma,
+            dma((2, sky_count)),
+            dma((2, freq_count)),
+            dma((2, channels, 2)),
+            dma((2, channels, 2)),
+            dma((2, channels, 2)),
+            dma((2, channels, 2)),
+            dma((len(STEPS), channels)),
+            dma((len(STEPS), channels)),
+        ],
+        compiler_params=pltpu.CompilerParams(
+            collective_id=1, has_side_effects=True, vmem_limit_bytes=48 * 2**20
+        ),
+        name="combine",
+    )(pieces, beam, labels)
 
 
 def shards(pieces, beam, destination, clip_tenths):
-    sky_count = lax.axis_size("sky")
-    piece_count, channels, block_size, _ = pieces.shape
-    tile_blocks = ROWB * COLB
-    capacity = max(2, 2 * piece_count // sky_count)
-    slot_total = sky_count * capacity
-    owners = destination // tile_blocks
-    numbering = jnp.arange(piece_count)
-    earlier = (owners[None, :] == owners[:, None]) & (numbering[None, :] < numbering[:, None])
-    position = jnp.sum(earlier.astype(jnp.int32), axis=1)
-    slot_index = owners * capacity + position
-    weighted = (beam[:, None].astype(F32) * pieces.astype(F32)).astype(BF16)
-    outgoing = jnp.zeros((slot_total, channels, block_size, block_size), BF16).at[slot_index].set(weighted)
-    beams_out = jnp.zeros((slot_total, block_size, block_size), BF16).at[slot_index].set(beam)
-    labels_out = jnp.full((slot_total,), -1, jnp.int32).at[slot_index].set(destination % tile_blocks)
-    arrived, beams_in, labels_in = (
-        lax.all_to_all(outgoing, "sky", split_axis=0, concat_axis=0, tiled=True),
-        lax.all_to_all(beams_out, "sky", split_axis=0, concat_axis=0, tiled=True),
-        lax.all_to_all(labels_out, "sky", split_axis=0, concat_axis=0, tiled=True),
-    )
-    onehot, coverage = owner_tables(beams_in, labels_in, tile_blocks)
-    tile_values = block_values(onehot, coverage, arrived)
-    combined = tile_values.reshape(ROWB, COLB, channels, block_size, block_size).transpose(2, 0, 3, 1, 4)
-    combined = combined.reshape(channels, ROWB * block_size, COLB * block_size)
-    forward, backward = neighbours("sky")
-    above = lax.ppermute(combined[:, -NEAR:], "sky", forward)
-    below = lax.ppermute(combined[:, :NEAR], "sky", backward)
-    tall = jnp.concatenate([combined, above, below], axis=1)
-    forward, backward = neighbours("freq")
-    low = lax.ppermute(tall[-EDGE:], "freq", forward)
-    high = lax.ppermute(tall[:EDGE], "freq", backward)
-    cpad = jnp.concatenate([low, tall, high], axis=0)
+    cpad = combine(pieces, beam, destination)
     smoothed, power = smooth_and_power(cpad)
     factor = clip_factors(power, clip_tenths)
     return scores(factor, smoothed)

time: 275 us -> 148 us (0.54)
  waiting for transfers between devices: 148 us -> 0 us
  Pallas kernels: 49.8 us -> 134 us
  starting transfers between devices: 32.1 us -> 0 us
  local copies, waits for them, and re-layouts: 26.8 us -> 14.2 us
  matrix products: 10.3 us -> 0 us
  other arithmetic: 5.52 us -> 0.01 us
    all_to_all x3 -> x0, waiting for transfers between devices: 128 us -> none  [the longest x1 123 us: shards(): lax.all_to_all(outgoing, 'sky', split_axis=0, concat_axis=0, tiled=True)]
    pallas_call x0 -> x1, Pallas kernels: none -> 83.2 us  [combine(): pl.pallas_call(functools.partial(combine_kernel, sky_count, freq_count),...]
    ppermute x4 -> x0, waiting for transfers between devices: 19.8 us -> none  [the longest x1 11 us: shards(): low = lax.ppermute(tall[-EDGE:], 'freq', forward)]
    all_to_all x3 -> x0, starting transfers between devices: 16.2 us -> none  [the longest x1 7.58 us: shards(): lax.all_to_all(labels_out, 'sky', split_axis=0, concat_axis=0, tiled=True)]
    ppermute x4 -> x0, starting transfers between devices: 15.9 us -> none  [the longest x1 11.4 us: shards(): low = lax.ppermute(tall[-EDGE:], 'freq', forward)]
    dot_general x2 -> x0, matrix products: 10.3 us -> none  [the longest x1 8.3 us: block_values(): jnp.einsum('bs,scyx->bcyx', onehot, arrived, preferred_element_type=F32)]
    scatter x3 -> x0, local copies, waits for them, and re-layouts: 8.01 us -> none  [the longest x1 5 us: shards(): jnp.zeros((slot_total, channels, block_size, block_size), BF16)]
    broadcast_in_dim x2 -> x1, local copies, waits for them, and re-layouts: 6.57 us -> 0.72 us  [combine(): labels = jnp.broadcast_to(destination[:, None], (piece_count, BLK))]
  transfers between devices with their start and end apart: 7 -> 0, of which waited for: 7 -> 0; matrix products, arithmetic and copies ran while one was open for 7% -> 0% of each run, Pallas kernels for 0% -> 0%
where the time goes in v2:
time: 148 us
  Pallas kernels  134 us (91%)
  local copies, waits for them, and re-layouts  14.2 us (10%)
    pallas_call x1, Pallas kernels, combine(): pl.pallas_call(functools.partial(combine_kernel, sky_count, freq_count),...  83.2 us
    pallas_call x1, Pallas kernels, smooth_and_power(): pl.pallas_call(smooth_kernel, grid=(KERNELS,), out_shape=(jax.ShapeDtypeS...  32.6 us
    unnamed x20, local copies, waits for them, and re-layouts  12.7 us
    pallas_call x1, Pallas kernels, clip_factors(): pl.pallas_call(functools.partial(factor_kernel, count), out_shape=jax.Sha...  10.5 us
    pallas_call x1, Pallas kernels, scores(): pl.pallas_call(score_kernel, grid=(BLK // NEAR,), out_shape=jax.ShapeDtyp...  7.37 us

profile of v2, /device:TPU:1, one launch (start us, length us, event | category | flops | bytes accessed | tf_op | source)
XLA Modules:
  0.0 147.9 jit_solution(10624887707052886222)
XLA Ops:
  0.0 0.7 broadcast_in_dim.6.label_ref
  0.7 0.0 copy-start.3
  0.7 1.6 %copy-done.3 = bf16[8,8,128,128]{3,2,1,0:T(8,128)(2,1)S(1)} copy-done((bf16[8,8,128,128]{3,2,1,0:T(8,128)(2,1)S(1)}, bf16[8,8,128,128]{3,2,1,0:T(8,128)(2,1)}, u32[]{:S(2)}) %copy-start.3) | copy-done | bytes 2097176
  2.3 0.0 copy-start.5
  2.3 0.9 copy-done.5
  3.3 0.0 copy-start.4
  3.3 0.0 copy-start.6
  3.3 83.2 %combine.1.cpad_ref = bf16[24,160,512]{2,1,0:T(8,128)(2,1)} custom-call(bf16[8,8,128,128]{3,2,1,0:T(8,128)(2,1)S(1)} %copy-done.3, bf16[8,128,128]{2,1,0:T(8,128)(2,1)S(1)} %copy-done.5, s32[8,128]{1,0:T(8,128)S(1)} %broadcast_in_dim.6.label_ref), custom_call_target="tpu_custom_call" | custom-call | tf_op jit(solution)/shard_map/combine/pallas_call | solution.py:570
  86.4 0.0 copy-done.4
  86.5 0.0 copy-done.6
  86.5 0.0 copy-start
  86.5 2.1 %copy-done = bf16[24,160,512]{2,1,0:T(8,128)(2,1)S(1)} copy-done((bf16[24,160,512]{2,1,0:T(8,128)(2,1)S(1)}, bf16[24,160,512]{2,1,0:T(8,128)(2,1)}, u32[]{:S(2)}) %copy-start) | copy-done | bytes 3932184
  88.6 32.6 %smooth_and_power.1 = (bf16[3,22,128,512]{3,2,1,0:T(8,128)(2,1)S(1)}, f32[8,128]{1,0:T(8,128)S(1)}) custom-call(bf16[24,160,512]{2,1,0:T(8,128)(2,1)S(1)} %copy-done, bf16[3,512,512]{2,1,0:T(8,128)(2,1)S(1)} %copy-done.4, bf16[3,128,160]{2,1,0:T(8,128)(2,1)S(1)} %copy-done.6), custom_call_target="tpu_custom_call" | custom-call | tf_op jit(solution)/shard_map/smooth_and_power/pallas_call | solution.py:112
  121.1 0.0 copy-start.1
  121.1 3.4 %copy-done.1 = bf16[3,22,128,512]{3,2,1,0:T(8,128)(2,1)} copy-done((bf16[3,22,128,512]{3,2,1,0:T(8,128)(2,1)}, bf16[3,22,128,512]{3,2,1,0:T(8,128)(2,1)S(1)}, u32[]{:S(2)}) %copy-start.1) | copy-done | bytes 8650776
  124.5 0.6 copy-done.8
  125.1 0.0 copy-done.9
  125.1 0.1 reshape.4
  125.2 0.6 broadcast_in_dim.15.clip_ref
  125.8 10.5 %clip_factors.1.factor_ref = f32[8,128]{1,0:T(8,128)} custom-call(f32[8,128]{1,0:T(8,128)} %copy-done.8, f32[8,128]{1,0:T(8,128)} %broadcast_in_dim.15.clip_ref), custom_call_target="tpu_custom_call" | custom-call | tf_op jit(solution)/shard_map/clip_factors/pallas_call | solution.py:178
  136.3 0.0 copy-start.2
  136.4 3.4 %copy-done.2 = bf16[3,22,128,512]{3,2,1,0:T(8,128)(2,1)S(1)} copy-done((bf16[3,22,128,512]{3,2,1,0:T(8,128)(2,1)S(1)}, bf16[3,22,128,512]{3,2,1,0:T(8,128)(2,1)}, u32[]{:S(2)}) %copy-start.2) | copy-done | bytes 8650776
  139.8 0.7 copy-done.7
  140.5 7.4 %scores.1 = f32[8,128,512]{2,1,0:T(8,128)} custom-call(f32[8,128]{1,0:T(8,128)S(1)} %copy-done.7, bf16[3,22,128,512]{3,2,1,0:T(8,128)(2,1)S(1)} %copy-done.2), custom_call_target="tpu_custom_call" | custom-call | tf_op jit(solution)/shard_map/scores/pallas_call | solution.py:211
  (5 shorter events, 0.0 us)
Async XLA Ops:
  0.7 1.6 %copy-start.3 = (bf16[8,8,128,128]{3,2,1,0:T(8,128)(2,1)S(1)}, bf16[8,8,128,128]{3,2,1,0:T(8,128)(2,1)}, u32[]{:S(2)}) copy-start(bf16[8,8,128,128]{3,2,1,0:T(8,128)(2,1)} %pieces_ref.1) | copy-start | bytes 6291460
  2.3 0.9 copy-start.5
  3.3 83.2 %copy-start.4 = (bf16[3,512,512]{2,1,0:T(8,128)(2,1)S(1)}, bf16[3,512,512]{2,1,0:T(8,128)(2,1)}, u32[]{:S(2)}) copy-start(bf16[3,512,512]{2,1,0:T(8,128)(2,1)} %constant.6.clone.across_ref) | copy-start | bytes 4718596
  3.3 83.2 %copy-start.6 = (bf16[3,128,160]{2,1,0:T(8,128)(2,1)S(1)}, bf16[3,128,160]{2,1,0:T(8,128)(2,1)}, u32[]{:S(2)}) copy-start(bf16[3,128,160]{2,1,0:T(8,128)(2,1)} %constant.7.clone.down_ref) | copy-start | bytes 368644
  86.5 2.1 %copy-start = (bf16[24,160,512]{2,1,0:T(8,128)(2,1)S(1)}, bf16[24,160,512]{2,1,0:T(8,128)(2,1)}, u32[]{:S(2)}) copy-start(bf16[24,160,512]{2,1,0:T(8,128)(2,1)} %combine.1.cpad_ref) | copy-start | bytes 11796484
  88.6 36.5 %copy-start.9 = (s32[3,4]{1,0:T(4,128)S(1)}, s32[3,4]{1,0:T(4,128)}, u32[]{:S(2)}) copy-start(s32[3,4]{1,0:T(4,128)} %param.9) | copy-start | bytes 148
  121.1 3.4 %copy-start.1 = (bf16[3,22,128,512]{3,2,1,0:T(8,128)(2,1)}, bf16[3,22,128,512]{3,2,1,0:T(8,128)(2,1)S(1)}, u32[]{:S(2)}) copy-start(bf16[3,22,128,512]{3,2,1,0:T(8,128)(2,1)S(1)} %get-tuple-element.8.smoothed_ref) | copy-start | bytes 25952260
  124.5 0.6 copy-start.8
  136.3 3.5 %copy-start.2 = (bf16[3,22,128,512]{3,2,1,0:T(8,128)(2,1)S(1)}, bf16[3,22,128,512]{3,2,1,0:T(8,128)(2,1)}, u32[]{:S(2)}) copy-start(bf16[3,22,128,512]{3,2,1,0:T(8,128)(2,1)} %copy-done.1) | copy-start | bytes 25952260
  139.8 0.7 copy-start.7

commit v3 on v2

v3 whole, which is shorter than its diff:
```python
import functools
import numpy as np
import ml_dtypes
import jax
import jax.numpy as jnp
from jax import lax
from jax.experimental import pallas as pl
from jax.experimental.pallas import tpu as pltpu
from jax.sharding import PartitionSpec as P

ROWB = 1
COLB = 4
BLK = 128
RIM = 8
EDGE = 7
KERNELS = 3
WIDTHS = 4
NEAR = 16
REGULARIZER = 0.05
EPSILON = 1e-06
KERNEL_FWHM = (3.0, 6.0, 9.0)
HALF_WIDTHS = (0, 1, 3, 7)
CELLS = 2048 * 512
WINDOW = 256
MESH = pl.DeviceIdType.MESH
VMEM = pltpu.VMEM
F32 = jnp.float32
BF16 = jnp.bfloat16


def band_constants():
    across, down = [], [[], []]
    for fwhm in KERNEL_FWHM:
        offsets = np.arange(-RIM, RIM + 1).astype(np.float32)
        sigma = np.float32(fwhm / 2.3548)
        taps = np.exp(-offsets * offsets / (np.float32(2.0) * sigma * sigma)).astype(ml_dtypes.bfloat16)

        def pick(distance):
            inside = np.abs(distance) <= RIM
            return np.where(inside, taps[np.clip(distance + RIM, 0, 2 * RIM)], taps.dtype.type(0))

        columns = np.arange(WINDOW)
        across.append(pick(columns[:, None] - columns[None, :]))
        rows = np.arange(BLK)
        away = np.full(RIM, 4 * BLK)
        above, below = np.arange(-RIM, 0), BLK + np.arange(RIM)
        for half, order in enumerate((lambda v: [v, away], lambda v: [away, v])):
            source = np.concatenate([rows] + order(above) + order(below))
            down[half].append(pick(source[None, :] - rows[:, None]))
    return jnp.asarray(np.stack(across)), jnp.asarray(np.stack([np.concatenate(half) for half in down]))


def box_sums(a):
    count = len(a) - 2 * EDGE
    two = {i: a[i] + a[i + 1] for i in range(4, 16)}
    three = {i: two[i] + a[i + 2] for i in range(6, 16)}
    four = {i: two[i] + two[i + 2] for i in range(4, 12)}
    own = four[7] + four[11]
    low = {6: a[6]}
    for i in range(5, -1, -1):
        low[i] = a[i] + low[i + 1]
    high = {1: a[15]}
    for i in range(2, 8):
        high[i] = high[i - 1] + a[i + 14]
    found = []
    for c in range(count):
        wide = own
        if c in low:
            wide = wide + low[c]
        if c in high:
            wide = wide + high[c]
        found.append((a[c + 7], three[c + 6], four[c + 4] + three[c + 8], wide))
    return found


SIDE = 4
GROUP = 4
PIECES = 8
DIAGONALS = ((1, 1), (1, -1), (-1, 1), (-1, -1))
EDGES = ((1, 0), (-1, 0)) + DIAGONALS
HALF = COLB // 2
ROWS = 64
SIDES = (1, -1)
ORIENTATIONS = (0, 1)


def whole_kernel(
    sky_count, freq_count, pieces_hbm, beam_hbm, destination_ref, clip_ref, across_ref, down_ref, out_ref,
    pieces_ref, beam_ref, label_ref, held, first_out, first_in, second_out, second_in, label_all, label_s,
    cover_out, cover_in, inverse, main, edge_out, edge_in, halfway, smoothed, acc, power_out, power_in, factor_v,
    factor_s,
    load_sems, label_sems, local_sems, cover_sems, inverse_sems, wave_sems, hop_sems, first_sems, second_sems,
    main_sems, edge_sems, power_sems,
):
    t, f = lax.axis_index("sky"), lax.axis_index("freq")
    x, y = t // SIDE, lax.rem(t, SIDE)
    load_pieces = pltpu.make_async_copy(pieces_hbm, pieces_ref, load_sems.at[0])
    load_beam = pltpu.make_async_copy(beam_hbm, beam_ref, load_sems.at[1])
    load_beam.start()
    load_pieces.start()
    barrier = pltpu.get_barrier_semaphore()

    def at(o, d):
        if o == 0:
            return lax.rem(x + d + SIDE, SIDE) * SIDE + y
        return x * SIDE + lax.rem(y + d + SIDE, SIDE)

    def remote(source, target, sems, where, sky, freq):
        return pltpu.make_async_remote_copy(
            src_ref=source, dst_ref=target, send_sem=sems.at[(0,) + where], recv_sem=sems.at[(1,) + where],
            device_id=(sky, freq), device_id_type=MESH,
        )

    def within(dt, df):
        good = None
        for value, delta, count in ((t, dt, sky_count), (f, df, freq_count)):
            if delta:
                here = value + delta
                one = (here >= 0) & (here < count)
                good = one if good is None else good & one
        return good

    def greet_sky(d, _):
        pl.semaphore_signal(barrier, 1, device_id=(lax.rem(t + d, sky_count), f), device_id_type=MESH)
        return 0

    def greet_freq(d, _):
        pl.semaphore_signal(barrier, 1, device_id=(t, lax.rem(f + d, freq_count)), device_id_type=MESH)
        return 0

    lax.fori_loop(1, sky_count, greet_sky, 0)
    lax.fori_loop(1, freq_count, greet_freq, 0)
    for dt, df in DIAGONALS:
        @pl.when(within(dt, df))
        def _():
            pl.semaphore_signal(barrier, 1, device_id=(t + dt, f + df), device_id_type=MESH)

    for p in range(PIECES):
        label_ref[p : p + 1, :] = jnp.full((1, BLK), destination_ref[p], jnp.int32)
    label_all[t] = label_ref[...]

    for edge, n in ((t == 0, 0), (t == sky_count - 1, 1)):
        @pl.when(edge)
        def _():
            for g in range(3):
                for i in range(GROUP):
                    edge_in[g, i, n] = jnp.zeros((NEAR, COLB * BLK), BF16)
    for edge, g in ((f == 0, 0), (f == freq_count - 1, 2)):
        @pl.when(edge)
        def _():
            edge_in[g] = jnp.zeros(edge_in.shape[1:], BF16)

            def clear(c, _):
                main[g * 2 * GROUP + c] = jnp.zeros(main.shape[1:], BF16)
                return 0

            lax.fori_loop(0, 2 * GROUP, clear, 0)

    load_beam.wait()
    load_pieces.wait()

    def weigh(c, _):
        for p in range(PIECES):
            value = beam_ref[p].astype(F32) * pieces_ref[p, c].astype(F32)
            held[c, 0, p] = value.astype(BF16)
        return 0

    lax.fori_loop(0, 2 * GROUP, weigh, 0)
    diagonals = jnp.int32(0)
    for dt, df in DIAGONALS:
        diagonals = diagonals + within(dt, df).astype(jnp.int32)
    pl.semaphore_wait(barrier, sky_count - 1 + freq_count - 1 + diagonals)

    def wave(o, i, side):
        c = o * GROUP + i
        n = (1 - side) // 2
        return remote(held.at[c, 0], held.at[c, 1 if side == 1 else 3], wave_sems, (c, n), at(o, side), f)

    def onward(o, i, side):
        c = o * GROUP + i
        n = (1 - side) // 2
        half = pl.ds(n * (PIECES // 2), PIECES // 2)
        return remote(
            held.at[c, 1 if side == 1 else 3, half], held.at[c, 2, half], hop_sems, (c, n), at(o, side), f
        )

    def first(o, i, side):
        c = o * GROUP + i
        n = (1 - side) // 2
        return remote(first_out.at[c, n], first_in.at[c, n], first_sems, (c, n), at(1 - o, side), f)

    def second(o, i, side):
        c = o * GROUP + i
        n = (1 - side) // 2
        return remote(second_out.at[c, n], second_in.at[c, n], second_sems, (c, n), at(1 - o, side), f)

    def label_copy(d):
        return remote(label_ref, label_all.at[t], label_sems, (d,), lax.rem(t + d, sky_count), f)

    def start_labels(d, _):
        label_copy(d).start()
        return 0

    lax.fori_loop(1, sky_count, start_labels, 0)
    for o in ORIENTATIONS:
        for side in SIDES:
            wave(o, 0, side).start()

    pair = pl.ds(pl.multiple_of((f // 2) * NEAR, NEAR), NEAR)
    squares = []
    for p in range(PIECES):
        both = beam_ref[p, pair, :].astype(F32)
        mine = jnp.where(lax.rem(f, 2) == 0, both[:8], both[8:])
        squares.append(mine * mine)
    labels = [jnp.broadcast_to(label_ref[p : p + 1, :], (8, BLK)) for p in range(PIECES)]

    def cover(tile, _):
        for b in range(COLB):
            found = jnp.zeros((8, BLK), F32)
            for p in range(PIECES):
                found = found + jnp.where(labels[p] == tile * COLB + b, squares[p], 0.0)
            cover_out[tile, b] = found
        return 0

    lax.fori_loop(0, sky_count, cover, 0)

    def cover_copy(d):
        other = lax.rem(t + d, sky_count)
        return remote(cover_out.at[other], cover_in.at[d], cover_sems, (d,), other, f)

    def start_cover(d, _):
        cover_copy(d).start()
        return 0

    lax.fori_loop(1, sky_count, start_cover, 0)
    for o in ORIENTATIONS:
        for side in SIDES:
            wave(o, 1, side).start()

    def finish_labels(d, _):
        label_copy(d).wait_send()
        source = lax.rem(t - d + sky_count, sky_count)
        remote(label_ref, label_all.at[source], label_sems, (d,), source, f).wait_recv()
        return 0

    lax.fori_loop(1, sky_count, finish_labels, 0)
    to_scalars = pltpu.make_async_copy(label_all, label_s, local_sems.at[0])
    to_scalars.start()

    def finish_cover(d, _):
        cover_copy(d).wait()
        return 0

    lax.fori_loop(1, sky_count, finish_cover, 0)
    coverage = cover_out[t] + REGULARIZER
    for d in range(1, sky_count):
        coverage = coverage + cover_in[d]
    inverse[f] = 1.0 / coverage

    def inverse_copy(d):
        return remote(inverse.at[f], inverse.at[f], inverse_sems, (d,), t, lax.rem(f + d, freq_count))

    def start_inverse(d, _):
        inverse_copy(d).start()
        return 0

    lax.fori_loop(1, freq_count, start_inverse, 0)
    to_scalars.wait()

    def finish_inverse(d, _):
        inverse_copy(d).wait_send()
        source = lax.rem(f - d + freq_count, freq_count)
        remote(inverse.at[source], inverse.at[source], inverse_sems, (d,), t, source).wait_recv()
        return 0

    def sums(o, c, d, rows):
        base = at(1 - o, d) * COLB

        def source(j, found):
            sky = at(o, -j)
            found = list(found)
            for p in range(PIECES):
                value = held[c, j, p, rows, :].astype(F32)
                label = label_s[sky, p, 0]
                for b in range(COLB):
                    found[b] = found[b] + jnp.where(label == base + b, 1.0, 0.0) * value
            return tuple(found)

        return list(lax.fori_loop(0, SIDE, source, tuple(jnp.zeros((ROWS, BLK), F32) for _ in range(COLB))))

    def by_rows(body):
        def chunk(r, _):
            body(pl.ds(pl.multiple_of(r * ROWS, ROWS), ROWS), r)
            return 0

        lax.fori_loop(0, BLK // ROWS, chunk, 0)

    def main_copy(c, df):
        own = 2 * GROUP + c
        return remote(main.at[own], main.at[own - 2 * GROUP * df], main_sems, (c, (1 - df) // 2), t, f + df)

    def edge_copy(i, m):
        dt, df = EDGES[m]
        n = (1 - dt) // 2
        return remote(edge_out.at[i, n], edge_in.at[1 - df, i, n], edge_sems, (i, m), t + dt, f + df)

    def smooth(i):
        for m, (dt, df) in enumerate(EDGES):
            @pl.when(within(-dt, -df))
            def _():
                edge_copy(i, m).wait_recv()
        for df in SIDES:
            @pl.when(within(0, -df))
            def _():
                for o in ORIENTATIONS:
                    main_copy(o * GROUP + i, df).wait_recv()
        for g in range(3):
            for o in ORIENTATIONS:
                tall = jnp.concatenate(
                    [main[g * 2 * GROUP + o * GROUP + i], edge_in[g, i, 0], edge_in[g, i, 1]], axis=0
                )
                found = jnp.dot(down_ref[o], tall, preferred_element_type=F32).astype(BF16)
                spot = (2 * g + o) * BLK
                for k in range(KERNELS):
                    halfway[k, spot : spot + BLK, :] = found[k * BLK : (k + 1) * BLK]
        lane = lax.broadcasted_iota(jnp.int32, (6 * BLK, BLK), 1)
        for k in range(KERNELS):
            matrix = across_ref[k]
            found = [
                jnp.dot(halfway[k, :, n * BLK : n * BLK + WINDOW], matrix, preferred_element_type=F32)
                for n in range(3)
            ]
            columns = (
                found[0][:, :BLK],
                jnp.where(lane < BLK - RIM, found[0][:, BLK:], found[1][:, :BLK]),
                jnp.where(lane >= RIM, found[2][:, :BLK], found[1][:, BLK:]),
                found[2][:, BLK:],
            )
            for n, value in enumerate(columns):
                value = value.astype(BF16)
                for g in range(3):
                    for o in ORIENTATIONS:
                        spot = (2 * g + o) * BLK
                        smoothed[k, g * 2 * GROUP + o * GROUP + i, :, n * BLK : (n + 1) * BLK] = value[spot : spot + BLK]

    def step(n, _):
        @pl.when(n < GROUP)
        def _():
            for o in ORIENTATIONS:
                for side in SIDES:
                    wave(o, n, side).wait_recv()
                    onward(o, n, side).start()

        @pl.when(n < GROUP - 2)
        def _():
            for o in ORIENTATIONS:
                for side in SIDES:
                    wave(o, n + 2, side).start()

        @pl.when((n >= 1) & (n < GROUP + 1))
        def _():
            i = n - 1
            for o in ORIENTATIONS:
                c = o * GROUP + i
                for side in SIDES:
                    onward(o, i, side).wait_recv()

                def far(rows, r):
                    found = sums(o, c, 2, rows)
                    for b in range(COLB):
                        first_out[c, b // HALF, b % HALF, rows, :] = found[b].astype(BF16)

                by_rows(far)
                for side in SIDES:
                    first(o, i, side).start()

        @pl.when((n >= 2) & (n < GROUP + 2))
        def _():
            i = n - 2
            for o in ORIENTATIONS:
                c = o * GROUP + i
                for m, side in enumerate(SIDES):
                    first(o, i, side).wait_recv()

                    def near(rows, r):
                        found = sums(o, c, side, rows)
                        for b in range(HALF):
                            found[m * HALF + b] = found[m * HALF + b] + first_in[c, m, b, rows, :].astype(F32)
                        for b in range(COLB):
                            second_out[c, m, b, rows, :] = found[b].astype(BF16)

                    by_rows(near)
                    second(o, i, side).start()

        @pl.when(n == 3)
        def _():
            lax.fori_loop(1, freq_count, finish_inverse, 0)

        @pl.when((n >= 3) & (n < GROUP + 3))
        def _():
            i = n - 3
            for o in ORIENTATIONS:
                c = o * GROUP + i
                for side in SIDES:
                    second(o, i, side).wait_recv()

                def own(rows, r):
                    found = sums(o, c, 0, rows)
                    for b in range(COLB):
                        value = found[b]
                        for m in range(2):
                            value = value + second_in[c, m, b, rows, :].astype(F32)
                        scale = jnp.concatenate([inverse[r * (ROWS // 8) + q, b] for q in range(ROWS // 8)], axis=0)
                        main[2 * GROUP + c, rows, b * BLK : (b + 1) * BLK] = (value * scale).astype(BF16)

                by_rows(own)
                for df in SIDES:
                    @pl.when(within(0, df))
                    def _():
                        main_copy(c, df).start()
            ends = [
                [main[2 * GROUP + o * GROUP + i, rows, :].astype(F32) for o in ORIENTATIONS]
                for rows in (slice(BLK - NEAR, BLK), slice(0, NEAR))
            ]
            edge_out[i, 0] = jnp.concatenate([value[RIM:] for value in ends[0]], axis=0).astype(BF16)
            edge_out[i, 1] = jnp.concatenate([value[:RIM] for value in ends[1]], axis=0).astype(BF16)
            for m, (dt, df) in enumerate(EDGES):
                @pl.when(within(dt, df))
                def _():
                    edge_copy(i, m).start()

        @pl.when(n >= 4)
        def _():
            smooth(n - 4)

        return 0

    lax.fori_loop(0, GROUP + 4, step, 0)

    channels = 2 * GROUP
    total = channels + 2 * EDGE
    lane = lax.broadcasted_iota(jnp.int32, (channels, BLK), 1)
    power = jnp.zeros((channels, BLK), F32)
    chunks = (BLK // NEAR) * COLB

    def layers(k, i):
        rows = pl.ds(pl.multiple_of((i // COLB) * NEAR, NEAR), NEAR)
        columns = pl.ds(pl.multiple_of(lax.rem(i, COLB) * BLK, BLK), BLK)
        return rows, columns, [smoothed[k, c + 1, rows, columns].astype(F32) for c in range(total)]

    for k in range(KERNELS):
        acc[...] = jnp.zeros_like(acc)

        def energy(i, _):
            _, _, a = layers(k, i)
            for c, found in enumerate(box_sums(a)):
                for w, item in enumerate(found):
                    square = item * item
                    acc[w, c] += square[:8] + square[8:]
            return 0

        lax.fori_loop(0, chunks, energy, 0)
        for w in range(WIDTHS):
            value = jnp.sum(jnp.sum(acc[w], axis=1), axis=1, keepdims=True)
            power = jnp.where(lane == k * WIDTHS + w, value, power)
    power_out[...] = power

    def power_copy(d):
        return remote(power_out, power_in.at[d], power_sems, (d,), lax.rem(t + d, sky_count), f)

    def start_power(d, _):
        power_copy(d).start()
        return 0

    def finish_power(d, _):
        power_copy(d).wait()
        return 0

    lax.fori_loop(1, sky_count, start_power, 0)

    def drain(i, _):
        for o in ORIENTATIONS:
            for side in SIDES:
                for copy in (wave, onward, first, second):
                    copy(o, i, side).wait_send()
        for m, (dt, df) in enumerate(EDGES):
            @pl.when(within(dt, df))
            def _():
                edge_copy(i, m).wait_send()
        for df in SIDES:
            @pl.when(within(0, df))
            def _():
                for o in ORIENTATIONS:
                    main_copy(o * GROUP + i, df).wait_send()
        return 0

    lax.fori_loop(0, GROUP, drain, 0)
    clip = jnp.ones((channels, BLK), jnp.int32)
    for k in range(KERNELS):
        for w in range(WIDTHS):
            clip = jnp.where(lane == k * WIDTHS + w, clip_ref[k, w], clip)
    lax.fori_loop(1, sky_count, finish_power, 0)
    power = power_out[...]
    for d in range(1, sky_count):
        power = power + power_in[d]
    noise = jnp.sqrt(power * (1.0 / CELLS) + EPSILON)
    factor_v[...] = 10.0 / (clip.astype(F32) * noise)
    factors = pltpu.make_async_copy(factor_v, factor_s, local_sems.at[1])
    factors.start()
    factors.wait()

    def score(i, _):
        best = [None] * channels
        for k in range(KERNELS):
            rows, columns, a = layers(k, i)
            for c, found in enumerate(box_sums(a)):
                for w, item in enumerate(found):
                    value = jnp.abs(item) * factor_s[c, k * WIDTHS + w]
                    best[c] = value if best[c] is None else jnp.maximum(best[c], value)
        for c, item in enumerate(best):
            out_ref[c, rows, columns] = item
        return 0

    lax.fori_loop(0, chunks, score, 0)


def shards(pieces, beam, destination, clip_tenths):
    sky_count, freq_count = lax.axis_size("sky"), lax.axis_size("freq")
    piece_count, channels = pieces.shape[:2]
    across, down = band_constants()
    dma = pltpu.SemaphoreType.DMA
    plane = (BLK, BLK)
    row = COLB * BLK
    return pl.pallas_call(
        functools.partial(whole_kernel, sky_count, freq_count),
        out_shape=jax.ShapeDtypeStruct((channels, BLK, row), F32),
        in_specs=[
            pl.BlockSpec(memory_space=pl.ANY),
            pl.BlockSpec(memory_space=pl.ANY),
            pl.BlockSpec(memory_space=pltpu.SMEM),
            pl.BlockSpec(memory_space=pltpu.SMEM),
            pl.BlockSpec(memory_space=VMEM),
            pl.BlockSpec(memory_space=VMEM),
        ],
        out_specs=pl.BlockSpec(memory_space=VMEM),
        scratch_shapes=[
            VMEM(pieces.shape, BF16),
            VMEM(beam.shape, BF16),
            VMEM((piece_count, BLK), jnp.int32),
            VMEM((channels, SIDE, piece_count) + plane, BF16),
            VMEM((channels, 2, HALF) + plane, BF16),
            VMEM((channels, 2, HALF) + plane, BF16),
            VMEM((channels, 2, COLB) + plane, BF16),
            VMEM((channels, 2, COLB) + plane, BF16),
            VMEM((sky_count, piece_count, BLK), jnp.int32),
            pltpu.SMEM((sky_count, piece_count, BLK), jnp.int32),
            VMEM((sky_count, COLB, 8, BLK), F32),
            VMEM((sky_count, COLB, 8, BLK), F32),
            VMEM((freq_count, COLB, 8, BLK), F32),
            VMEM((3 * channels, BLK, row), BF16),
            VMEM((GROUP, 2, NEAR, row), BF16),
            VMEM((3, GROUP, 2, NEAR, row), BF16),
            VMEM((KERNELS, 6 * BLK, row), BF16),
            VMEM((KERNELS, 3 * channels, BLK, row), BF16),
            VMEM((WIDTHS, channels, 8, BLK), F32),
            VMEM((channels, BLK), F32),
            VMEM((sky_count, channels, BLK), F32),
            VMEM((channels, BLK), F32),
            pltpu.SMEM((channels, BLK), F32),
            dma((2,)),
            dma((2, sky_count)),
            dma((2,)),
            dma((2, sky_count)),
            dma((2, freq_count)),
            dma((2, channels, 2)),
            dma((2, channels, 2)),
            dma((2, channels, 2)),
            dma((2, channels, 2)),
            dma((2, channels, 2)),
            dma((2, GROUP, len(EDGES))),
            dma((2, sky_count)),
        ],
        compiler_params=pltpu.CompilerParams(
            collective_id=1, has_side_effects=True, vmem_limit_bytes=56 * 2**20
        ),
        name="whole",
    )(pieces, beam, destination, clip_tenths, across, down)


def solution(mesh):
    return jax.shard_map(
        shards,
        mesh=mesh,
        in_specs=(P("sky", "freq", None, None), P("sky", None, None), P("sky"), P()),
        out_specs=P("freq", "sky", None),
        check_vma=False,
    )
```

time: 148 us -> 108 us (0.73)
  Pallas kernels: 134 us -> 105 us
  local copies, waits for them, and re-layouts: 14.2 us -> 3.08 us
    pallas_call x4 -> x1, Pallas kernels: 134 us -> 105 us  [shards(): pl.pallas_call(functools.partial(whole_kernel, sky_count, freq_count), ou...]
    unnamed x20 -> x1, local copies, waits for them, and re-layouts: 12.7 us -> 3.08 us
where the time goes in v3:
time: 108 us
  Pallas kernels  105 us (97%)
  local copies, waits for them, and re-layouts  3.08 us (3%)
    pallas_call x1, Pallas kernels, shards(): pl.pallas_call(functools.partial(whole_kernel, sky_count, freq_count), ou...  105 us
    unnamed x1, local copies, waits for them, and re-layouts  3.08 us

profile of v3, /device:TPU:1, one launch (start us, length us, event | category | flops | bytes accessed | tf_op | source)
XLA Modules:
  0.0 108.1 jit_solution(11721683265287046499)
XLA Ops:
  0.0 105.0 %whole.1 = f32[8,128,512]{2,1,0:T(8,128)} custom-call(bf16[8,8,128,128]{3,2,1,0:T(8,128)(2,1)} %pieces_hbm.1, bf16[8,128,128]{2,1,0:T(8,128)(2,1)} %beam_hbm.1, s32[8]{0:T(128)} %destination_ref.1, s32[3,4]{1,0:T(4,128)} %clip_ref.1, bf16[3,256,256]{2,1,0:T(8,128)(2,1)} %constant.4.clone.across_ref, bf16[2,384,160]{2,1,0:T(8,128)(2,1)} %constant.5.clone.down_ref), custom_call_target="tpu_custom_call" | custom-call | tf_op jit(solution)/shard_map/whole/pallas_call | solution.py:534
  105.1 3.1 %copy.8 = f32[8,128,512]{2,1,0:T(8,128)} copy(f32[8,128,512]{2,1,0:T(8,128)} %whole.1) | data formatting | bytes 4194304

commit v4 on v3

v4 whole, which is shorter than its diff:
```python
import functools
import numpy as np
import ml_dtypes
import jax
import jax.numpy as jnp
from jax import lax
from jax.experimental import pallas as pl
from jax.experimental.pallas import tpu as pltpu
from jax.sharding import PartitionSpec as P

ROWB = 1
COLB = 4
BLK = 128
RIM = 8
EDGE = 7
KERNELS = 3
WIDTHS = 4
NEAR = 16
TALL = BLK + NEAR
REGULARIZER = 0.05
EPSILON = 1e-06
KERNEL_FWHM = (3.0, 6.0, 9.0)
HALF_WIDTHS = (0, 1, 3, 7)
CELLS = 2048 * 512
WINDOW = 256
MESH = pl.DeviceIdType.MESH
VMEM = pltpu.VMEM
F32 = jnp.float32
BF16 = jnp.bfloat16


def band_constants():
    across, down = [], []
    for fwhm in KERNEL_FWHM:
        offsets = np.arange(-RIM, RIM + 1).astype(np.float32)
        sigma = np.float32(fwhm / 2.3548)
        taps = np.exp(-offsets * offsets / (np.float32(2.0) * sigma * sigma)).astype(ml_dtypes.bfloat16)

        def pick(distance):
            inside = np.abs(distance) <= RIM
            return np.where(inside, taps[np.clip(distance + RIM, 0, 2 * RIM)], taps.dtype.type(0))

        columns = np.arange(WINDOW)
        across.append(pick(columns[:, None] - columns[None, :]))
        rows = np.arange(BLK)
        source = np.concatenate([rows, np.arange(-RIM, 0), BLK + np.arange(RIM)])
        down.append(pick(source[None, :] - rows[:, None]))
    return jnp.asarray(np.stack(across)), jnp.asarray(np.concatenate(down))


def box_sums(a):
    count = len(a) - 2 * EDGE
    two = {i: a[i] + a[i + 1] for i in range(4, 16)}
    three = {i: two[i] + a[i + 2] for i in range(6, 16)}
    four = {i: two[i] + two[i + 2] for i in range(4, 12)}
    own = four[7] + four[11]
    low = {6: a[6]}
    for i in range(5, -1, -1):
        low[i] = a[i] + low[i + 1]
    high = {1: a[15]}
    for i in range(2, 8):
        high[i] = high[i - 1] + a[i + 14]
    found = []
    for c in range(count):
        wide = own
        if c in low:
            wide = wide + low[c]
        if c in high:
            wide = wide + high[c]
        found.append((a[c + 7], three[c + 6], four[c + 4] + three[c + 8], wide))
    return found


SIDE = 4
GROUP = 4
PIECES = 8
DOUBLINGS = (1, 2, 4, 8)
HALF = COLB // 2
ROWS = 64
SIDES = (1, -1)
ORIENTATIONS = (0, 1)


def whole_kernel(
    sky_count, freq_count, pieces_hbm, beam_hbm, destination_ref, clip_ref, across_hbm, down_hbm, out_hbm,
    beam_ref, across_ref, down_ref, held, first_out, first_in, second_out, second_in, label_all, label_s,
    share, cover_out, cover_in, inverse, near_part, own_part, stage, spot_s, block_s, main, halfway, smoothed, acc, power_out, power_in,
    splat, out_ref,
    load_sems, label_sems, local_sems, share_sems, cover_sems, inverse_sems, wave_sems, hop_sems, first_sems,
    second_sems, main_sems, power_sems, out_sems,
):
    t, f = lax.axis_index("sky"), lax.axis_index("freq")
    x, y = t // SIDE, lax.rem(t, SIDE)
    barrier = pltpu.get_barrier_semaphore()

    def at(o, d):
        if o == 0:
            return lax.rem(x + d + SIDE, SIDE) * SIDE + y
        return x * SIDE + lax.rem(y + d + SIDE, SIDE)

    def remote(source, target, sems, where, sky, freq):
        return pltpu.make_async_remote_copy(
            src_ref=source, dst_ref=target, send_sem=sems.at[(0,) + where], recv_sem=sems.at[(1,) + where],
            device_id=(sky, freq), device_id_type=MESH,
        )

    def within(dt, df):
        good = None
        for value, delta, count in ((t, dt, sky_count), (f, df, freq_count)):
            if delta:
                here = value + delta
                one = (here >= 0) & (here < count)
                good = one if good is None else good & one
        return good

    def partner(size):
        return f + size * (1 - 2 * lax.rem(f // size, 2))

    def greet(sky, freq):
        pl.semaphore_signal(barrier, 1, device_id=(sky, freq), device_id_type=MESH)

    for o in ORIENTATIONS:
        for d in range(1, SIDE):
            greet(at(o, d), f)
    for size in DOUBLINGS:
        greet(t, partner(size))
    others = ((lax.rem(f, 2) == 1) & within(0, 1), (lax.rem(f, 2) == 0) & within(0, -1))
    more = jnp.int32(0)
    for here, df in ((others[0], 1), (others[1], -1)):
        more = more + here.astype(jnp.int32)

        @pl.when(here)
        def _():
            greet(t, f + df)

    load_beam = pltpu.make_async_copy(beam_hbm, beam_ref, load_sems.at[0])
    load_across = pltpu.make_async_copy(across_hbm, across_ref, load_sems.at[1])
    load_down = pltpu.make_async_copy(down_hbm, down_ref, load_sems.at[2])
    loads = [
        pltpu.make_async_copy(pieces_hbm.at[:, c], held.at[c, 0], load_sems.at[3 + c]) for c in range(2 * GROUP)
    ]
    load_beam.start()
    for load in loads:
        load.start()
    load_across.start()
    load_down.start()

    for p in range(PIECES):
        for o in ORIENTATIONS:
            label_all[o, 0, p : p + 1, :] = jnp.full((1, BLK), destination_ref[p], jnp.int32)

    for edge, g in ((f == 0, 0), (f == freq_count - 1, 2)):
        @pl.when(edge)
        def _():
            def clear(c, _):
                main[g * 2 * GROUP + c] = jnp.zeros(main.shape[1:], BF16)
                return 0

            lax.fori_loop(0, 2 * GROUP, clear, 0)

    load_beam.wait()
    pair = pl.ds(pl.multiple_of((f // 2) * NEAR, NEAR), NEAR)

    def mine(p):
        both = beam_ref[p, pair, :].astype(F32)
        return jnp.where(lax.rem(f, 2) == 0, both[:8], both[8:])

    for q in range(PIECES // 2):
        share[0, q] = jnp.concatenate([mine(2 * q), mine(2 * q + 1)], axis=0).astype(BF16)
    for load in loads:
        load.wait()

    def weigh(c, _):
        for p in range(PIECES):
            value = beam_ref[p].astype(F32) * held[c, 0, p].astype(F32)
            held[c, 0, p] = value.astype(BF16)
        return 0

    lax.fori_loop(0, 2 * GROUP, weigh, 0)
    pl.semaphore_wait(barrier, 2 * (SIDE - 1) + len(DOUBLINGS) + more)

    def channel_of(o, i):
        return GROUP + i if o else lax.rem(i + 1, GROUP)

    def wave(o, i, side):
        c = channel_of(o, i)
        n = (1 - side) // 2
        return remote(held.at[c, 0], held.at[c, 1 if side == 1 else 3], wave_sems, (c, n), at(o, side), f)

    def onward(o, i, side):
        c = channel_of(o, i)
        n = (1 - side) // 2
        half = pl.ds(n * (PIECES // 2), PIECES // 2)
        return remote(
            held.at[c, 1 if side == 1 else 3, half], held.at[c, 2, half], hop_sems, (c, n), at(o, side), f
        )

    def first(o, i, side):
        c = channel_of(o, i)
        n = (1 - side) // 2
        return remote(first_out.at[c, n], first_in.at[c, n], first_sems, (c, n), at(1 - o, side), f)

    def second(o, i, side):
        c = channel_of(o, i)
        n = (1 - side) // 2
        return remote(second_out.at[c, n], second_in.at[c, n], second_sems, (c, n), at(1 - o, side), f)

    def label_copy(o, d):
        return remote(label_all.at[o, 0], label_all.at[o, d], label_sems, (o, d), at(o, d), f)

    def share_copy(d):
        return remote(share.at[0], share.at[d], share_sems, (d,), at(0, d), f)

    for d in range(1, SIDE):
        share_copy(d).start()
        for o in ORIENTATIONS:
            label_copy(o, d).start()
    for o in ORIENTATIONS:
        for side in SIDES:
            wave(o, 0, side).start()

    for d in range(1, SIDE):
        for o in ORIENTATIONS:
            label_copy(o, d).wait()
        share_copy(d).wait()
    to_scalars = pltpu.make_async_copy(label_all, label_s, local_sems.at[0])
    to_scalars.start()

    aside = jnp.where(f < freq_count // 2, COLB, -COLB)

    def cover(d, _):
        base = at(1, d) * COLB
        found = [jnp.zeros((8, BLK), F32) for _ in range(2 * COLB)]
        for j in range(SIDE):
            for p in range(PIECES):
                value = share[j, p // 2].astype(F32)[(p % 2) * 8 : (p % 2) * 8 + 8]
                square = value * value
                label = jnp.broadcast_to(label_all[0, j, p : p + 1, :], (8, BLK))
                for b in range(COLB):
                    found[b] = found[b] + jnp.where(label == base + b, square, 0.0)
                    found[COLB + b] = found[COLB + b] + jnp.where(label == base + aside + b, square, 0.0)
        for b in range(2 * COLB):
            cover_out[d, b] = found[b]
        return 0

    lax.fori_loop(0, SIDE, cover, 0)

    def cover_copy(d):
        return remote(cover_out.at[d], cover_in.at[d], cover_sems, (d,), at(1, d), f)

    for d in range(1, SIDE):
        cover_copy(d).start()
    for o in ORIENTATIONS:
        for side in SIDES:
            wave(o, 1, side).start()
    for d in range(1, SIDE):
        cover_copy(d).wait()
    coverage = cover_out[0] + REGULARIZER
    for d in range(1, SIDE):
        coverage = coverage + cover_in[d]
    inverse[f] = 1.0 / coverage

    def spread(s, arrives):
        size = DOUBLINGS[s]
        other = partner(size)
        base = (other if arrives else f) // size * size
        span = inverse.at[pl.ds(base, size)]
        return remote(span, span, inverse_sems, (s,), t, other)

    spread(0, False).start()
    to_scalars.wait()
    load_across.wait()
    load_down.wait()

    for o in ORIENTATIONS:
        def tabulate(n, _):
            d, j = n // SIDE, lax.rem(n, SIDE)
            base = at(1 - o, d) * COLB
            spots = [jnp.int32(0), jnp.int32(0)]
            blocks = [jnp.int32(-1), jnp.int32(-1)]
            for p in range(PIECES):
                block = label_s[o, j, p, 0] - base
                inside = (block >= 0) & (block < COLB)
                again = inside & (blocks[0] >= 0)
                fresh = inside & (blocks[0] < 0)
                spots[1] = jnp.where(again, p, spots[1])
                blocks[1] = jnp.where(again, block, blocks[1])
                spots[0] = jnp.where(fresh, p, spots[0])
                blocks[0] = jnp.where(fresh, block, blocks[0])
            for k in range(2):
                spot_s[o, d, j, k] = spots[k]
                block_s[o, d, j, k] = blocks[k]
            return 0

        lax.fori_loop(0, SIDE * SIDE, tabulate, 0)

    def chosen(label, block):
        return jnp.where(label == block, 1.0, 0.0)

    def lay_out(o, c):
        def one(n, _):
            stage[o, n] = held[c, n // PIECES, lax.rem(n, PIECES)]
            return 0

        lax.fori_loop(0, SIDE * PIECES, one, 0)

    def sums(o, d, emit):
        base = at(1 - o, d) * COLB
        step_d = d % SIDE

        def chunk(r, _):
            rows = pl.ds(pl.multiple_of(r * ROWS, ROWS), ROWS)
            found = [jnp.zeros((ROWS, BLK), F32) for _ in range(COLB)]
            for j in range(SIDE):
                for k in range(2):
                    value = stage[o, j * PIECES + spot_s[o, step_d, j, k], rows, :].astype(F32)
                    label = block_s[o, step_d, j, k]
                    for b in range(COLB):
                        found[b] = found[b] + chosen(label, b) * value
            emit(rows, found, r)
            return 0

        lax.fori_loop(0, BLK // ROWS, chunk, 0)

        def beside(j, found):
            found = list(found)
            for p in range(PIECES):
                above = stage[o, j * PIECES + p, BLK - NEAR :, :].astype(F32)[RIM:]
                below = stage[o, j * PIECES + p, :NEAR, :].astype(F32)[:RIM]
                label = label_s[o, j, p, 0]
                for b in range(COLB):
                    found[b] = found[b] + chosen(label, base - COLB + b) * above
                    found[COLB + b] = found[COLB + b] + chosen(label, base + COLB + b) * below
            return tuple(found)

        found = lax.fori_loop(0, SIDE, beside, tuple(jnp.zeros((RIM, BLK), F32) for _ in range(2 * COLB)))
        emit(pl.ds(BLK, NEAR), [jnp.concatenate([found[b], found[COLB + b]], axis=0) for b in range(COLB)], None)

    def by_rows(body):
        def chunk(r, _):
            body(pl.ds(pl.multiple_of(r * ROWS, ROWS), ROWS), r)
            return 0

        lax.fori_loop(0, BLK // ROWS, chunk, 0)
        body(pl.ds(BLK, NEAR), None)

    def main_copy(o, i, df):
        c = channel_of(o, i)
        own = 2 * GROUP + c
        return remote(main.at[own], main.at[own - 2 * GROUP * df], main_sems, (c, (1 - df) // 2), t, f + df)

    def main_needed(o, i, df):
        return i < GROUP - 1 if o == (1 - df) // 2 else True

    def each_main(i, body, sign):
        for o in ORIENTATIONS:
            for df in SIDES:
                @pl.when(within(0, sign * df) & main_needed(o, i, df))
                def _():
                    body(main_copy(o, i, df))

    def smooth(i, chosen):
        for m, (g, o) in enumerate(chosen):
            tall = main[g * 2 * GROUP + channel_of(o, i)]
            found = jnp.dot(down_ref[...], tall, preferred_element_type=F32).astype(BF16)
            for k in range(KERNELS):
                halfway[k, m * BLK : (m + 1) * BLK, :] = found[k * BLK : (k + 1) * BLK]
        height = len(chosen) * BLK
        lane = lax.broadcasted_iota(jnp.int32, (height, BLK), 1)
        for k in range(KERNELS):
            matrix = across_ref[k]
            found = [
                jnp.dot(halfway[k, :height, n * BLK : n * BLK + WINDOW], matrix, preferred_element_type=F32)
                for n in range(3)
            ]
            columns = (
                found[0][:, :BLK],
                jnp.where(lane < BLK - RIM, found[0][:, BLK:], found[1][:, :BLK]),
                jnp.where(lane >= RIM, found[2][:, :BLK], found[1][:, BLK:]),
                found[2][:, BLK:],
            )
            for n, value in enumerate(columns):
                value = value.astype(BF16)
                for m, (g, o) in enumerate(chosen):
                    smoothed[k, g * 2 * GROUP + channel_of(o, i), :, n * BLK : (n + 1) * BLK] = (
                        value[m * BLK : (m + 1) * BLK]
                    )

    def wait_around(i):
        each_main(i, lambda copy: copy.wait_recv(), -1)

    def step(n, _):
        @pl.when(n < GROUP)
        def _():
            for o in ORIENTATIONS:
                for side in SIDES:
                    wave(o, n, side).wait_recv()
                    onward(o, n, side).start()

        @pl.when(n < GROUP - 2)
        def _():
            for o in ORIENTATIONS:
                for side in SIDES:
                    wave(o, n + 2, side).start()

        for s in range(len(DOUBLINGS)):
            @pl.when(n == s)
            def _():
                spread(s, False).wait_send()
                spread(s, True).wait_recv()
                if s + 1 < len(DOUBLINGS):
                    spread(s + 1, False).start()

        @pl.when(n >= 3)
        def _():
            i = n - 3
            for o in ORIENTATIONS:
                c = channel_of(o, i)
                for side in SIDES:
                    second(o, i, side).wait_recv()

                def own(rows, r):
                    for b in range(COLB):
                        value = own_part[o, b, rows, :]
                        for m in range(2):
                            value = value + second_in[c, m, b, rows, :].astype(F32)
                        if r is None:
                            scale = [inverse[freq_count - 1, COLB + b], inverse[0, COLB + b]]
                        else:
                            scale = [inverse[r * (ROWS // 8) + q, b] for q in range(ROWS // 8)]
                        value = value * jnp.concatenate(scale, axis=0)
                        main[2 * GROUP + c, rows, b * BLK : (b + 1) * BLK] = value.astype(BF16)

                by_rows(own)
            each_main(i, lambda copy: copy.start(), 1)

        @pl.when((n >= 2) & (n < GROUP + 2))
        def _():
            i = n - 2
            for o in ORIENTATIONS:
                c = channel_of(o, i)
                for m, side in enumerate(SIDES):
                    first(o, i, side).wait_recv()

                    def near(rows, r):
                        for b in range(COLB):
                            value = near_part[o, m, b, rows, :]
                            if b // HALF == m:
                                value = value + first_in[c, m, b % HALF, rows, :].astype(F32)
                            second_out[c, m, b, rows, :] = value.astype(BF16)

                    by_rows(near)
                    second(o, i, side).start()
            for o in ORIENTATIONS:
                def keep_own(rows, found, r):
                    for b in range(COLB):
                        own_part[o, b, rows, :] = found[b]

                sums(o, 0, keep_own)

        @pl.when((n >= 1) & (n < GROUP + 1))
        def _():
            i = n - 1
            for o in ORIENTATIONS:
                c = channel_of(o, i)
                for side in SIDES:
                    onward(o, i, side).wait_recv()

                def far(rows, found, r):
                    for b in range(COLB):
                        first_out[c, b // HALF, b % HALF, rows, :] = found[b].astype(BF16)

                lay_out(o, c)
                sums(o, 2, far)
                for side in SIDES:
                    first(o, i, side).start()
            for o in ORIENTATIONS:
                for m, side in enumerate(SIDES):
                    def keep_near(rows, found, r):
                        for b in range(COLB):
                            near_part[o, m, b, rows, :] = found[b]

                    sums(o, side, keep_near)

        @pl.when(n >= 3)
        def _():
            smooth(n - 3, ((1, 0), (1, 1)))

        @pl.when(n >= 4)
        def _():
            wait_around(n - 4)
            smooth(n - 4, ((0, 0), (0, 1), (2, 0), (2, 1)))

        return 0

    lax.fori_loop(0, GROUP + 3, step, 0)
    wait_around(GROUP - 1)
    smooth(GROUP - 1, ((0, 1), (2, 0)))

    channels = 2 * GROUP
    total = channels + 2 * EDGE
    lane = lax.broadcasted_iota(jnp.int32, (channels, BLK), 1)
    chunks = (BLK // NEAR) * COLB

    def layers(k, i):
        rows = pl.ds(pl.multiple_of((i // COLB) * NEAR, NEAR), NEAR)
        columns = pl.ds(pl.multiple_of(lax.rem(i, COLB) * BLK, BLK), BLK)
        return rows, columns, [smoothed[k, c + 1, rows, columns].astype(F32) for c in range(total)]

    def power_copy(k, o, d):
        return remote(power_out.at[k, o], power_in.at[k, o, d], power_sems, (k, o, d), at(o, d), f)

    def send_power(k, o, value):
        power_out[k, o] = value
        for d in range(1, SIDE):
            power_copy(k, o, d).start()

    def gathered(k, o):
        for d in range(1, SIDE):
            power_copy(k, o, d).wait()
        value = power_out[k, o]
        for d in range(1, SIDE):
            value = value + power_in[k, o, d]
        return value

    def take_power(k):
        acc[...] = jnp.zeros_like(acc)

        def energy(i, _):
            _, _, a = layers(k, i)
            for c, found in enumerate(box_sums(a)):
                for w, item in enumerate(found):
                    square = item * item
                    acc[w, c] += square[:8] + square[8:]
            return 0

        lax.fori_loop(0, chunks, energy, 0)
        power = jnp.zeros((channels, BLK), F32)
        for w in range(WIDTHS):
            value = jnp.sum(jnp.sum(acc[w], axis=1), axis=1, keepdims=True)
            power = jnp.where(lane == w, value, power)
        return power

    def take_scores(k):
        clip = jnp.ones((channels, BLK), jnp.int32)
        for w in range(WIDTHS):
            clip = jnp.where(lane == w, clip_ref[k, w], clip)
        noise = jnp.sqrt(gathered(k, 1) * (1.0 / CELLS) + EPSILON)
        factor = 10.0 / (clip.astype(F32) * noise)
        for c in range(channels):
            for w in range(WIDTHS):
                splat[c, w] = jnp.broadcast_to(factor[c : c + 1, w : w + 1], (8, BLK))

        def score(i, _):
            rows, columns, a = layers(k, i)
            for c, found in enumerate(box_sums(a)):
                best = None if k == 0 else out_ref[c, rows, columns].reshape(2, 8, BLK)
                for w, item in enumerate(found):
                    value = jnp.abs(item).reshape(2, 8, BLK) * splat[c, w]
                    best = value if best is None else jnp.maximum(best, value)
                out_ref[c, rows, columns] = best.reshape(NEAR, BLK)
            if k == KERNELS - 1:
                @pl.when(lax.rem(i, COLB) == COLB - 1)
                def _():
                    deliver(i // COLB).start()
            return 0

        lax.fori_loop(0, chunks, score, 0)

    def deliver(r):
        rows = pl.ds(pl.multiple_of(r * NEAR, NEAR), NEAR)
        return pltpu.make_async_copy(out_ref.at[:, rows], out_hbm.at[:, rows], out_sems.at[r])

    send_power(0, 0, take_power(0))
    power = take_power(1)
    send_power(0, 1, gathered(0, 0))
    send_power(1, 0, power)
    power = take_power(2)
    send_power(1, 1, gathered(1, 0))
    send_power(2, 0, power)
    take_scores(0)
    send_power(2, 1, gathered(2, 0))
    take_scores(1)

    def drain(i, _):
        for o in ORIENTATIONS:
            for side in SIDES:
                for copy in (wave, onward, first, second):
                    copy(o, i, side).wait_send()
        each_main(i, lambda copy: copy.wait_send(), 1)
        return 0

    lax.fori_loop(0, GROUP, drain, 0)
    take_scores(2)

    def delivered(r, _):
        deliver(r).wait()
        return 0

    lax.fori_loop(0, BLK // NEAR, delivered, 0)


def shards(pieces, beam, destination, clip_tenths):
    sky_count, freq_count = lax.axis_size("sky"), lax.axis_size("freq")
    piece_count, channels = pieces.shape[:2]
    across, down = band_constants()
    dma = pltpu.SemaphoreType.DMA
    plane, tall = (BLK, BLK), (TALL, BLK)
    row = COLB * BLK
    return pl.pallas_call(
        functools.partial(whole_kernel, sky_count, freq_count),
        out_shape=jax.ShapeDtypeStruct((channels, BLK, row), F32),
        in_specs=[
            pl.BlockSpec(memory_space=pl.ANY),
            pl.BlockSpec(memory_space=pl.ANY),
            pl.BlockSpec(memory_space=pltpu.SMEM),
            pl.BlockSpec(memory_space=pltpu.SMEM),
            pl.BlockSpec(memory_space=pl.ANY),
            pl.BlockSpec(memory_space=pl.ANY),
        ],
        out_specs=pl.BlockSpec(memory_space=pl.ANY),
        scratch_shapes=[
            VMEM(beam.shape, BF16),
            VMEM(across.shape, BF16),
            VMEM(down.shape, BF16),
            VMEM((channels, SIDE, piece_count) + plane, BF16),
            VMEM((channels, 2, HALF) + tall, BF16),
            VMEM((channels, 2, HALF) + tall, BF16),
            VMEM((channels, 2, COLB) + tall, BF16),
            VMEM((channels, 2, COLB) + tall, BF16),
            VMEM((2, SIDE, piece_count, BLK), jnp.int32),
            pltpu.SMEM((2, SIDE, piece_count, BLK), jnp.int32),
            VMEM((SIDE, piece_count // 2, NEAR, BLK), BF16),
            VMEM((SIDE, 2 * COLB, 8, BLK), F32),
            VMEM((SIDE, 2 * COLB, 8, BLK), F32),
            VMEM((freq_count, 2 * COLB, 8, BLK), F32),
            VMEM((2, 2, COLB) + tall, F32),
            VMEM((2, COLB) + tall, F32),
            VMEM((2, SIDE * piece_count) + plane, BF16),
            pltpu.SMEM((2, SIDE, SIDE, 2), jnp.int32),
            pltpu.SMEM((2, SIDE, SIDE, 2), jnp.int32),
            VMEM((3 * channels, TALL, row), BF16),
            VMEM((KERNELS, 4 * BLK, row), BF16),
            VMEM((KERNELS, 3 * channels, BLK, row), BF16),
            VMEM((WIDTHS, channels, 8, BLK), F32),
            VMEM((KERNELS, 2, channels, BLK), F32),
            VMEM((KERNELS, 2, SIDE, channels, BLK), F32),
            VMEM((channels, WIDTHS, 8, BLK), F32),
            VMEM((channels, BLK, row), F32),
            dma((3 + channels,)),
            dma((2, 2, SIDE)),
            dma((1,)),
            dma((2, SIDE)),
            dma((2, SIDE)),
            dma((2, len(DOUBLINGS))),
            dma((2, channels, 2)),
            dma((2, channels, 2)),
            dma((2, channels, 2)),
            dma((2, channels, 2)),
            dma((2, channels, 2)),
            dma((2, KERNELS, 2, SIDE)),
            dma((BLK // NEAR,)),
        ],
        compiler_params=pltpu.CompilerParams(
            collective_id=1, has_side_effects=True, vmem_limit_bytes=60 * 2**20
        ),
        name="whole",
    )(pieces, beam, destination, clip_tenths, across, down)


def solution(mesh):
    return jax.shard_map(
        shards,
        mesh=mesh,
        in_specs=(P("sky", "freq", None, None), P("sky", None, None), P("sky"), P()),
        out_specs=P("freq", "sky", None),
        check_vma=False,
    )
```

time: 108 us -> 97.4 us (0.902)
  Pallas kernels: 105 us -> 94.2 us
    pallas_call x1, Pallas kernels: 105 us -> 94.2 us  [shards(): pl.pallas_call(functools.partial(whole_kernel, sky_count, freq_count), ou...]
where the time goes in v4:
time: 97.4 us; the launch traced here: 97.3 us
  Pallas kernels  94.2 us (97%)
  local copies, waits for them, and re-layouts  3.08 us (3%)
    pallas_call x1, Pallas kernels, shards(): pl.pallas_call(functools.partial(whole_kernel, sky_count, freq_count), ou...  94.2 us
    unnamed x1, local copies, waits for them, and re-layouts  3.08 us

profile of v4, /device:TPU:1, one launch (start us, length us, event | category | flops | bytes accessed | tf_op | source)
XLA Modules:
  0.0 97.3 jit_solution(11238647865333430946)
XLA Ops:
  0.0 94.2 %whole.1 = f32[8,128,512]{2,1,0:T(8,128)} custom-call(bf16[8,8,128,128]{3,2,1,0:T(8,128)(2,1)} %pieces_hbm.1, bf16[8,128,128]{2,1,0:T(8,128)(2,1)} %beam_hbm.1, s32[8]{0:T(128)} %destination_ref.1, s32[3,4]{1,0:T(4,128)} %clip_ref.1, bf16[3,256,256]{2,1,0:T(8,128)(2,1)} %constant.4.clone.across_hbm, bf16[384,144]{1,0:T(8,128)(2,1)} %constant.5.clone.down_hbm), custom_call_target="tpu_custom_call" | custom-call | tf_op jit(solution)/shard_map/whole/pallas_call | solution.py:610
  94.2 3.1 %copy.8 = f32[8,128,512]{2,1,0:T(8,128)} copy(f32[8,128,512]{2,1,0:T(8,128)} %whole.1) | data formatting | bytes 4194304

commit v5 on v4

--- a/solution.py
+++ b/solution.py
@@ -79,6 +79,7 @@
 ROWS = 64
 SIDES = (1, -1)
 ORIENTATIONS = (0, 1)
+ORDER = ((1, 2, 3, 0), (4, 5, 6, 7))
 
 
 def whole_kernel(
@@ -140,8 +141,9 @@
         pltpu.make_async_copy(pieces_hbm.at[:, c], held.at[c, 0], load_sems.at[3 + c]) for c in range(2 * GROUP)
     ]
     load_beam.start()
-    for load in loads:
-        load.start()
+    for i in range(GROUP):
+        for o in ORIENTATIONS:
+            loads[ORDER[o][i]].start()
     load_across.start()
     load_down.start()
 
@@ -149,15 +151,6 @@
         for o in ORIENTATIONS:
             label_all[o, 0, p : p + 1, :] = jnp.full((1, BLK), destination_ref[p], jnp.int32)
 
-    for edge, g in ((f == 0, 0), (f == freq_count - 1, 2)):
-        @pl.when(edge)
-        def _():
-            def clear(c, _):
-                main[g * 2 * GROUP + c] = jnp.zeros(main.shape[1:], BF16)
-                return 0
-
-            lax.fori_loop(0, 2 * GROUP, clear, 0)
-
     load_beam.wait()
     pair = pl.ds(pl.multiple_of((f // 2) * NEAR, NEAR), NEAR)
 
@@ -167,16 +160,19 @@
 
     for q in range(PIECES // 2):
         share[0, q] = jnp.concatenate([mine(2 * q), mine(2 * q + 1)], axis=0).astype(BF16)
-    for load in loads:
-        load.wait()
-
-    def weigh(c, _):
-        for p in range(PIECES):
-            value = beam_ref[p].astype(F32) * held[c, 0, p].astype(F32)
-            held[c, 0, p] = value.astype(BF16)
-        return 0
-
-    lax.fori_loop(0, 2 * GROUP, weigh, 0)
+
+    def weigh(i):
+        for o in ORIENTATIONS:
+            loads[ORDER[o][i]].wait()
+
+            def one(p, _):
+                value = beam_ref[p].astype(F32) * held[ORDER[o][i], 0, p].astype(F32)
+                held[ORDER[o][i], 0, p] = value.astype(BF16)
+                return 0
+
+            lax.fori_loop(0, PIECES, one, 0)
+
+    weigh(0)
     pl.semaphore_wait(barrier, 2 * (SIDE - 1) + len(DOUBLINGS) + more)
 
     def channel_of(o, i):
@@ -250,9 +246,22 @@
 
     for d in range(1, SIDE):
         cover_copy(d).start()
+    weigh(1)
     for o in ORIENTATIONS:
         for side in SIDES:
             wave(o, 1, side).start()
+    weigh(2)
+    weigh(3)
+
+    for edge, g in ((f == 0, 0), (f == freq_count - 1, 2)):
+        @pl.when(edge)
+        def _():
+            def clear(c, _):
+                main[g * 2 * GROUP + c] = jnp.zeros(main.shape[1:], BF16)
+                return 0
+
+            lax.fori_loop(0, 2 * GROUP, clear, 0)
+
     for d in range(1, SIDE):
         cover_copy(d).wait()
     coverage = cover_out[0] + REGULARIZER

time: 97.4 us -> 97.4 us (level)
  no operation moved by 1% of the time
where the time goes in v5:
time: 97.4 us; the launch traced here: 97.3 us
  Pallas kernels  94.2 us (97%)
  local copies, waits for them, and re-layouts  3.08 us (3%)
    pallas_call x1, Pallas kernels, shards(): pl.pallas_call(functools.partial(whole_kernel, sky_count, freq_count), ou...  94.2 us
    unnamed x1, local copies, waits for them, and re-layouts  3.08 us

profile of v5, /device:TPU:1, one launch (start us, length us, event | category | flops | bytes accessed | tf_op | source)
XLA Modules:
  0.0 97.3 jit_solution(2812306801319671429)
XLA Ops:
  0.0 94.2 %whole.1 = f32[8,128,512]{2,1,0:T(8,128)} custom-call(bf16[8,8,128,128]{3,2,1,0:T(8,128)(2,1)} %pieces_hbm.1, bf16[8,128,128]{2,1,0:T(8,128)(2,1)} %beam_hbm.1, s32[8]{0:T(128)} %destination_ref.1, s32[3,4]{1,0:T(4,128)} %clip_ref.1, bf16[3,256,256]{2,1,0:T(8,128)(2,1)} %constant.4.clone.across_hbm, bf16[384,144]{1,0:T(8,128)(2,1)} %constant.5.clone.down_hbm), custom_call_target="tpu_custom_call" | custom-call | tf_op jit(solution)/shard_map/whole/pallas_call | solution.py:619
  94.2 3.1 %copy.8 = f32[8,128,512]{2,1,0:T(8,128)} copy(f32[8,128,512]{2,1,0:T(8,128)} %whole.1) | data formatting | bytes 4194304
